TPU v7x, 512 devices: a whole 4x8x8 slice. The times are simulated.
512 devices in a mesh: ctx: 64 (over z, y_hi, core), tp: 8 (over x, y_lo).
Axes of the slice: x: 4, y: 8 (y_hi: 4, y_lo: 2; y = y_hi * 2 + y_lo), z: 8, core: 2. Of those that a mesh axis runs over, the one named last changes fastest.
Arguments:
- queries: bfloat16 [12288, 4096], P('ctx', 'tp'), may hold values from -21 to 21
- keys: bfloat16 [12288, 1024], P('ctx', 'tp'), may hold values from -6 to 6
- values: bfloat16 [12288, 1024], P('ctx', 'tp'), may hold values from -6 to 6
- row_route: int32 [12288], P('ctx'), may hold values from 0 to 12287, as said below
- lengths: int32 [16], replicated, may hold values from 1 to 3072, 12288 in all
Outputs:
- attended: bfloat16 [12288, 4096], P('ctx', 'tp')
Inputs may be any that keep to these rules, and one draw needn't show every extreme that they name: `row_route`: A permutation of the output rows. The rows of one loader device bound for one rank (output rows r * 192 to (r + 1) * 192 - 1) number at most 6, exactly 6 for some rank; every loader device sends the same multiset of counts over the ranks, and every rank receives that multiset.
All inputs are finite; a program needn't handle non-finite values.
Results may differ from a plain program's by a relative error of at most 0.0065.
Values may be sent and summed in bfloat16 or wider, within the bound.
No kernel may reach another device: no remote copies, remote signals or barrier semaphores. Data moves between devices by JAX's collectives and lax.ppermute only.
A program may use at most 128 MiB of HBM per device.

v0:
```python
import jax
import jax.numpy as jnp
from jax import lax
from jax.sharding import PartitionSpec as P

HEAD_WIDTH = 128


def slot_position(row_ids, tok_dev, ranks_count):
    half_rows = tok_dev // 2
    owner = row_ids // tok_dev
    slot_id = row_ids - owner * tok_dev
    return jnp.where(
        slot_id < half_rows,
        owner * half_rows + slot_id,
        (2 * ranks_count - 1 - owner) * half_rows + slot_id - half_rows,
    )


def document_of(positions, lengths):
    boundary = jnp.cumsum(lengths)
    return jnp.sum((positions[:, None] >= boundary[None, :]).astype(jnp.int32), axis=1)


def local(queries, keys, values, row_route, lengths):
    ranks_count = lax.axis_size("ctx")
    my_index = lax.axis_index("ctx")
    tok_dev = queries.shape[0]
    feature_width = queries.shape[1]
    kv_heads = keys.shape[1] // HEAD_WIDTH
    query_groups = feature_width // (HEAD_WIDTH * kv_heads)
    capacity = 2 * tok_dev // ranks_count
    target = row_route // tok_dev
    slot_id = row_route - target * tok_dev
    onehot = (target[:, None] == jnp.arange(ranks_count, dtype=jnp.int32)[None, :]).astype(
        jnp.int32
    )
    before = jnp.cumsum(onehot, axis=0) - onehot
    ordinal = jnp.sum(before * onehot, axis=1)
    where_to = target * capacity + ordinal

    def pack_rows(row_data):
        return (
            jnp.zeros((ranks_count * capacity,) + row_data.shape[1:], row_data.dtype)
            .at[where_to]
            .set(row_data)
        )

    slot_buffer = jnp.full((ranks_count * capacity,), -1, jnp.int32).at[where_to].set(slot_id)

    def unpack_rows(row_data, slot_ids):
        drop_index = jnp.where(slot_ids >= 0, slot_ids, tok_dev)
        return (
            jnp.zeros((tok_dev,) + row_data.shape[1:], row_data.dtype)
            .at[drop_index]
            .set(row_data, mode="drop")
        )

    my_rows = my_index * tok_dev + jnp.arange(tok_dev, dtype=jnp.int32)
    query_pos = slot_position(my_rows, tok_dev, ranks_count)
    query_doc = document_of(query_pos, lengths)
    score_scale = HEAD_WIDTH ** (-0.5)
    got_queries, got_keys, got_values, got_slots = (
        lax.all_to_all(pack_rows(queries), "ctx", split_axis=0, concat_axis=0, tiled=True),
        lax.all_to_all(pack_rows(keys), "ctx", split_axis=0, concat_axis=0, tiled=True),
        lax.all_to_all(pack_rows(values), "ctx", split_axis=0, concat_axis=0, tiled=True),
        lax.all_to_all(slot_buffer, "ctx", split_axis=0, concat_axis=0, tiled=True),
    )
    local_queries = unpack_rows(got_queries, got_slots)
    local_keys = unpack_rows(got_keys, got_slots)
    local_values = unpack_rows(got_values, got_slots)
    query_heads = local_queries.reshape(tok_dev, kv_heads, query_groups, HEAD_WIDTH)
    pieces = (
        lax.all_gather(local_keys, "ctx", axis=0, tiled=True),
        lax.all_gather(local_values, "ctx", axis=0, tiled=True),
    )
    key_rows = jnp.arange(pieces[0].shape[0], dtype=jnp.int32)
    key_piece = pieces[0]
    value_piece = pieces[1]
    key_pos = slot_position(key_rows, tok_dev, ranks_count)
    best_score = jnp.full((kv_heads, query_groups, tok_dev), -1e30, jnp.float32)
    key_doc = document_of(key_pos, lengths)
    allowed = (query_doc[:, None] == key_doc[None, :]) & (key_pos[None, :] <= query_pos[:, None])
    heads_of_key = key_piece.reshape(key_piece.shape[0], kv_heads, HEAD_WIDTH)
    heads_of_value = value_piece.reshape(value_piece.shape[0], kv_heads, HEAD_WIDTH)
    scores = (
        jnp.einsum("tkgd,skd->kgts", query_heads, heads_of_key, preferred_element_type=jnp.float32)
        * score_scale
    )
    masked = jnp.where(allowed[None, None], scores, -1e30)
    new_best = jnp.maximum(best_score, jnp.max(masked, axis=3))
    weight = jnp.where(allowed[None, None], jnp.exp(masked - new_best[..., None]), 0.0)
    new_total = jnp.sum(weight, axis=3)
    new_acc = jnp.einsum(
        "kgts,skd->kgtd",
        weight.astype(jnp.bfloat16),
        heads_of_value,
        preferred_element_type=jnp.float32,
    )
    result = (new_best, new_total, new_acc)
    best_score, running_total, accumulated = result
    output = accumulated / running_total[..., None]
    return output.transpose(2, 0, 1, 3).reshape(tok_dev, feature_width).astype(jnp.bfloat16)


def solution(mesh):
    placed = (P("ctx", "tp"), P("ctx", "tp"), P("ctx", "tp"), P("ctx"), P())
    return jax.shard_map(
        local, mesh=mesh, in_specs=placed, out_specs=P("ctx", "tp"), check_vma=False
    )
```

profile of v0, /device:TPU:1, one launch (start us, length us, event | category | flops | bytes accessed | tf_op | source)
XLA Modules:
  0.0 255.1 jit_solution(15681184749573438938)
XLA Ops:
  6.5 0.7 multiply_subtract_fusion
  7.3 0.6 reduce-window.19
  7.9 0.2 slice_reduce_fusion
  8.1 0.1 bitcast_bitcast_fusion
  8.2 1.2 scatter_custom_fusion
  9.5 0.7 all_to_all.32
  10.2 17.6 %all-to-all-start = ((s32[64,6,1]{1,2,0:T(1,128)}), s32[64,6,1]{1,2,0:T(1,128)S(1)}, u32[]{:S(2)}, u32[]{:S(2)}) async-start(s32[64,6,1]{1,2,0:T(1,128)} %bitcast.2), calls=%async_computation | async-start | bytes 65536 | tf_op jit(solution)/shard_map/all_to_all | solution.py:67
  27.8 1.3 scatter_custom_fusion.1
  29.2 0.7 all_to_all.35
  29.9 9.8 %all-to-all-done = s32[64,6,1]{1,2,0:T(1,128)S(1)} async-done(((s32[64,6,1]{1,2,0:T(1,128)}), s32[64,6,1]{1,2,0:T(1,128)S(1)}, u32[]{:S(2)}, u32[]{:S(2)}) %all-to-all-start) | async-done | bytes 1568 | tf_op jit(solution)/shard_map/all_to_all | solution.py:67
  39.6 4.7 %all-to-all-start.1 = ((bf16[64,6,128]{2,1,0:T(8,128)(2,1)}), bf16[64,6,128]{2,1,0:T(8,128)(2,1)S(1)}, u32[]{:S(2)}, u32[]{:S(2)}) async-start(bf16[64,6,128]{2,1,0:T(8,128)(2,1)} %all_to_all.35), calls=%async_computation.1 | async-start | bytes 262144 | tf_op jit(solution)/shard_map/all_to_all | solution.py:65
  44.3 0.0 all-gather.3.cloned.1.call-start
  44.4 0.6 broadcast.290
  45.0 0.8 reduce.10
  45.7 0.1 all_to_all.34
  45.9 11.7 %all-to-all-done.1 = bf16[64,6,128]{2,1,0:T(8,128)(2,1)S(1)} async-done(((bf16[64,6,128]{2,1,0:T(8,128)(2,1)}), bf16[64,6,128]{2,1,0:T(8,128)(2,1)S(1)}, u32[]{:S(2)}, u32[]{:S(2)}) %all-to-all-start.1) | async-done | bytes 98336 | tf_op jit(solution)/shard_map/all_to_all | solution.py:65
  57.6 2.0 scatter_custom_fusion.2
  59.6 0.0 all-gather.3.cloned.1.call-update
  59.6 1.3 scatter_custom_fusion.5
  61.0 0.7 all_to_all.41
  61.7 4.5 %all-to-all-start.3 = ((bf16[64,6,128]{2,1,0:T(8,128)(2,1)}), bf16[64,6,128]{2,1,0:T(8,128)(2,1)S(1)}, u32[]{:S(2)}, u32[]{:S(2)}) async-start(bf16[64,6,128]{2,1,0:T(8,128)(2,1)} %all_to_all.41), calls=%async_computation.3 | async-start | bytes 262144 | tf_op jit(solution)/shard_map/all_to_all | solution.py:66
  66.2 1.8 scatter_custom_fusion.3
  68.0 0.9 all_to_all.38
  68.9 0.7 copy.18
  69.6 0.1 reduce.2
  69.8 0.1 convert_reduce_fusion.1
  69.9 0.2 convert_reduce_fusion
  70.2 10.0 %all-to-all-done.3 = bf16[64,6,128]{2,1,0:T(8,128)(2,1)S(1)} async-done(((bf16[64,6,128]{2,1,0:T(8,128)(2,1)}), bf16[64,6,128]{2,1,0:T(8,128)(2,1)S(1)}, u32[]{:S(2)}, u32[]{:S(2)}) %all-to-all-start.3) | async-done | bytes 98336 | tf_op jit(solution)/shard_map/all_to_all | solution.py:66
  80.1 4.5 %all-to-all-start.2 = ((bf16[64,6,512]{2,1,0:T(8,128)(2,1)}), bf16[64,6,512]{2,1,0:T(8,128)(2,1)S(1)}, u32[]{:S(2)}, u32[]{:S(2)}) async-start(bf16[64,6,512]{2,1,0:T(8,128)(2,1)} %all_to_all.38), calls=%async_computation.2 | async-start | bytes 1048576 | tf_op jit(solution)/shard_map/all_to_all | solution.py:64
  84.6 0.0 all-gather.5.cloned.1.call-start
  84.7 2.0 scatter_custom_fusion.6
  86.7 0.0 all-gather.5.cloned.1.call-update
  86.8 1.9 compare_and_fusion
  88.7 15.4 %all-to-all-done.2 = bf16[64,6,512]{2,1,0:T(8,128)(2,1)S(1)} async-done(((bf16[64,6,512]{2,1,0:T(8,128)(2,1)}), bf16[64,6,512]{2,1,0:T(8,128)(2,1)S(1)}, u32[]{:S(2)}, u32[]{:S(2)}) %all-to-all-start.2) | async-done | bytes 393248 | tf_op jit(solution)/shard_map/all_to_all | solution.py:64
  104.0 0.1 reshape.278
  104.2 2.0 scatter_custom_fusion.4
  106.2 38.1 %all-gather.3.cloned.1.call-done = bf16[12288,128]{1,0:T(8,128)(2,1)} async-done(((bf16[192,128]{1,0:T(8,128)(2,1)}), bf16[12288,128]{1,0:T(8,128)(2,1)}) %all-gather.3.cloned.1.call-update) | async-done | bytes 3145744 | tf_op jit(solution)/shard_map/all_gather | solution.py:74
  144.2 18.0 %fusion = (f32[4,192]{1,0:T(4,128)S(1)}, f32[12288,192,4]{0,1,2:T(8,128)}) fusion(pred[192,12288]{1,0:T(8,128)(4,1)S(1)} %compare_and_fusion, bf16[12288,128]{1,0:T(8,128)(2,1)} %all-gather.3.cloned.1.call-done, bf16[192,512]{1,0:T(8,128)(2,1)S(1)} %scatter_custom_fusion.4), kind=kOutput, calls=%fused_computation.9 | convolution fusion | flops 2444229888 | bytes 43453440 | tf_op jit(solution)/shard_map/tkgd,skd->kgts/dot_general | solution.py:87
  162.3 18.1 %fusion.1 = f32[4,192]{1,0:T(4,128)S(1)} fusion(f32[12288,192,4]{0,1,2:T(8,128)} %get-tuple-element.8, f32[4,192]{1,0:T(4,128)S(1)} %broadcast_maximum_fusion, pred[192,12288]{1,0:T(8,128)(4,1)S(1)} %compare_and_fusion), kind=kLoop, calls=%fused_computation.10 | loop fusion | flops 47185152 | bytes 40114176 | tf_op jit(solution)/shard_map/reduce_sum | solution.py:93
  180.4 49.3 %all-gather.5.cloned.1.call-done = bf16[12288,128]{1,0:T(8,128)(2,1)} async-done(((bf16[192,128]{1,0:T(8,128)(2,1)}), bf16[12288,128]{1,0:T(8,128)(2,1)}) %all-gather.5.cloned.1.call-update) | async-done | bytes 3145744 | tf_op jit(solution)/shard_map/all_gather | solution.py:75
  229.7 17.7 %fusion.20 = bf16[192,1,4,128]{3,0,2,1:T(8,128)(2,1)S(1)} fusion(bf16[12288,128]{1,0:T(8,128)(2,1)} %all-gather.5.cloned.1.call-done, f32[12288,192,4]{0,1,2:T(8,128)} %get-tuple-element.8, f32[4,192]{1,0:T(4,128)S(1)} %broadcast_maximum_fusion, pred[192,12288]{1,0:T(8,128)(4,1)S(1)} %compare_and_fusion, f32[4,192]{1,0:T(4,128)S(1)} %fusion.1), kind=kOutput, calls=%fused_computation.21 | convolution fusion | flops 2463301632 | bytes 43456512 | tf_op jit(solution)/shard_map/kgts,skd->kgtd/dot_general | solution.py:94
  247.4 0.2 copy.23
  247.6 0.7 copy.37
  (13 shorter events, 0.3 us)
Async XLA Ops:
  10.2 29.4 %all-to-all-start = ((s32[64,6,1]{1,2,0:T(1,128)}), s32[64,6,1]{1,2,0:T(1,128)S(1)}, u32[]{:S(2)}, u32[]{:S(2)}) async-start(s32[64,6,1]{1,2,0:T(1,128)} %bitcast.2), calls=%async_computation | async-start | bytes 65536 | tf_op jit(solution)/shard_map/all_to_all | solution.py:67
  39.6 17.9 %all-to-all-start.1 = ((bf16[64,6,128]{2,1,0:T(8,128)(2,1)}), bf16[64,6,128]{2,1,0:T(8,128)(2,1)S(1)}, u32[]{:S(2)}, u32[]{:S(2)}) async-start(bf16[64,6,128]{2,1,0:T(8,128)(2,1)} %all_to_all.35), calls=%async_computation.1 | async-start | bytes 262144 | tf_op jit(solution)/shard_map/all_to_all | solution.py:65
  44.3 99.9 %all-gather.3.cloned.1.call-start = ((), (), s32[]{:S(2)}) async-start(), calls=%async_computation.4 | async-start | bytes 3194880 | tf_op jit(solution)/shard_map/all_gather | solution.py:74
  61.7 18.5 %all-to-all-start.3 = ((bf16[64,6,128]{2,1,0:T(8,128)(2,1)}), bf16[64,6,128]{2,1,0:T(8,128)(2,1)S(1)}, u32[]{:S(2)}, u32[]{:S(2)}) async-start(bf16[64,6,128]{2,1,0:T(8,128)(2,1)} %all_to_all.41), calls=%async_computation.3 | async-start | bytes 262144 | tf_op jit(solution)/shard_map/all_to_all | solution.py:66
  80.1 23.9 %all-to-all-start.2 = ((bf16[64,6,512]{2,1,0:T(8,128)(2,1)}), bf16[64,6,512]{2,1,0:T(8,128)(2,1)S(1)}, u32[]{:S(2)}, u32[]{:S(2)}) async-start(bf16[64,6,512]{2,1,0:T(8,128)(2,1)} %all_to_all.38), calls=%async_computation.2 | async-start | bytes 1048576 | tf_op jit(solution)/shard_map/all_to_all | solution.py:64
  84.6 145.1 %all-gather.5.cloned.1.call-start = ((), (), s32[]{:S(2)}) async-start(), calls=%async_computation.5 | async-start | bytes 3194880 | tf_op jit(solution)/shard_map/all_gather | solution.py:75
Sparse Core Ops, SparseCore 0:
  59.8 84.4 all-gather.2
  147.6 82.0 all-gather.4
where the time goes:
time: 256 us; the launch traced here: 255 us
  waiting for transfers between devices  134 us (52%)
  matrix products  35.8 us (14%)
  starting transfers between devices  31.4 us (12%)
  other arithmetic  22.9 us (9%)
  local copies, waits for them, and re-layouts  17.4 us (7%)
  between operations  13.6 us (5%)
    all_gather x1, waiting for transfers between devices, local(): lax.all_gather(local_values, 'ctx', axis=0, tiled=True)  49.3 us
    all_gather x1, waiting for transfers between devices, local(): lax.all_gather(local_keys, 'ctx', axis=0, tiled=True)  38.1 us
    reduce_sum x1, other arithmetic, local(): new_total = jnp.sum(weight, axis=3)  18.1 us
    dot_general x1, matrix products, local(): jnp.einsum('tkgd,skd->kgts', query_heads, heads_of_key, preferred_element...  18 us
    dot_general x1, matrix products, local(): jnp.einsum('kgts,skd->kgtd', weight.astype(jnp.bfloat16), heads_of_value,...  17.7 us
    all_to_all x1, starting transfers between devices, local(): lax.all_to_all(slot_buffer, 'ctx', split_axis=0, concat_axis=0, tiled=True)  17.6 us
    all_to_all x1, waiting for transfers between devices, local(): lax.all_to_all(pack_rows(queries), 'ctx', split_axis=0, concat_axis=0, ti...  15.4 us
    all_to_all x1, waiting for transfers between devices, local(): lax.all_to_all(pack_rows(keys), 'ctx', split_axis=0, concat_axis=0, tiled...  11.7 us
  transfers between devices with their start and end apart: 6, of which 6 were waited for; matrix products, arithmetic and copies ran while one was open for 19% of the time, Pallas kernels for 0%

commit v1 on v0

v1 whole, which is shorter than its diff:
```python
import functools
import math

import jax
import jax.numpy as jnp
from jax import lax
from jax.experimental import pallas as pl
from jax.experimental.pallas import tpu as pltpu
from jax.sharding import PartitionSpec as P

HEAD_WIDTH = 128
CAP = 12
SLOTS = 16
NEG = -1e30
VMEM = pl.BlockSpec(memory_space=pltpu.VMEM)
SMEM = pl.BlockSpec(memory_space=pltpu.SMEM)


def iota(shape, dim):
    return lax.broadcasted_iota(jnp.int32, shape, dim)


def pack_kernel(n, route_ref, k_ref, v_ref, kv_ref, pick_ref):
    tok = k_ref.shape[0]
    half = tok // 2
    rows = n * SLOTS
    route = route_ref[...]
    owner = jnp.zeros_like(route)
    owner = ((route.astype(jnp.float32) + 0.5) * (1.0 / tok)).astype(jnp.int32)
    slot = route - owner * tok
    pos = jnp.where(slot < half, owner * half + slot, (2 * n - 1 - owner) * half + slot - half)
    chunk = ((pos.astype(jnp.float32) + 0.5) * (1.0 / tok)).astype(jnp.int32)
    place = pos - chunk * tok
    square = (tok, tok)
    down, across = iota(square, 0), iota(square, 1)
    chunk_rows = jnp.broadcast_to(chunk, square)
    chunk_col = jnp.sum(jnp.where(down == across, chunk_rows, 0), axis=1, keepdims=True)
    earlier = jnp.where((chunk_col == chunk_rows) & (down < across), 1, 0)
    order = jnp.sum(earlier, axis=0, keepdims=True)
    where_to = chunk * SLOTS + order
    wide = (rows, tok)
    line = iota(wide, 0)
    one, zero = jnp.float32(1), jnp.float32(0)
    pick = jnp.where(line == jnp.broadcast_to(where_to, wide), one, zero).astype(jnp.bfloat16)
    pick_ref[...] = pick
    mark = jnp.where(line == jnp.broadcast_to(chunk * SLOTS + CAP, wide), one, zero).astype(
        jnp.bfloat16
    )
    lanes = (HEAD_WIDTH, tok)
    places = jnp.where(
        iota(lanes, 0) == jnp.broadcast_to(order, lanes),
        jnp.broadcast_to(place + 1, lanes).astype(jnp.float32),
        zero,
    ).astype(jnp.bfloat16)
    packed_k = jnp.dot(pick, k_ref[...], preferred_element_type=jnp.float32)
    packed_k += lax.dot_general(
        mark, places, (((1,), (1,)), ((), ())), preferred_element_type=jnp.float32
    )
    kv_ref[:, :HEAD_WIDTH] = packed_k.astype(jnp.bfloat16)
    kv_ref[:, HEAD_WIDTH:] = jnp.dot(
        pick, v_ref[...], preferred_element_type=jnp.float32
    ).astype(jnp.bfloat16)


def unpack_kernel(n, got_ref, kv_ref, pick_ref):
    tok = kv_ref.shape[0]
    rows = n * SLOTS
    one, zero = jnp.float32(1), jnp.float32(0)
    tall = (n, rows)
    chooser = jnp.where(iota(tall, 1) == iota(tall, 0) * SLOTS + CAP, one, zero).astype(
        jnp.bfloat16
    )
    places = jnp.dot(chooser, got_ref[:, :HEAD_WIDTH], preferred_element_type=jnp.float32)
    lanes = (HEAD_WIDTH, rows)
    spread = jnp.where((iota(lanes, 1) & (SLOTS - 1)) == iota(lanes, 0), one, zero).astype(
        jnp.bfloat16
    )
    across = jnp.dot(places.astype(jnp.bfloat16), spread, preferred_element_type=jnp.float32)
    mine = iota(tall, 1) - iota(tall, 0) * SLOTS
    place = jnp.sum(
        jnp.where((mine >= 0) & (mine < CAP), across, zero), axis=0, keepdims=True
    )
    wide = (tok, rows)
    pick = jnp.where(
        (iota(wide, 0) + 1).astype(jnp.float32) == jnp.broadcast_to(place, wide), one, zero
    ).astype(jnp.bfloat16)
    pick_ref[...] = pick
    kv_ref[...] = jnp.dot(pick, got_ref[...], preferred_element_type=jnp.float32).astype(
        jnp.bfloat16
    )


def attend_kernel(
    groups, lengths_ref, index_ref, pick_ref, q_ref, own_ref, *rest
):
    far_refs, (first_ref, second_ref, heads_ref) = rest[:4], rest[4:]
    tok = pick_ref.shape[0]
    half = tok // 2
    span = 2 * tok
    index = index_ref[0]
    chip = index // 2
    scale = HEAD_WIDTH ** (-0.5) * math.log2(math.e)

    for g in range(groups):
        heads_ref[g * tok : (g + 1) * tok, :] = jnp.dot(
            pick_ref[...],
            q_ref[:, g * HEAD_WIDTH : (g + 1) * HEAD_WIDTH],
            preferred_element_type=jnp.float32,
        ).astype(jnp.bfloat16)

    wide = (tok, span)
    query_pos = index * tok + iota(wide, 0)
    start = jnp.zeros(wide, jnp.int32)
    first_start = jnp.int32(0)
    end = jnp.int32(0)
    for i in range(lengths_ref.shape[0]):
        end = end + lengths_ref[i]
        start = jnp.where(query_pos >= end, end, start)
        first_start = jnp.where(index * tok >= end, end, first_start)

    def block(keys, values, base, state, last):
        key_pos = base + iota(wide, 1)
        allowed = key_pos >= start
        if last:
            allowed = allowed & (key_pos <= query_pos)
        out = []
        for g in range(groups):
            s = lax.dot_general(
                heads_ref[g * tok : (g + 1) * tok, :],
                keys,
                (((1,), (1,)), ((), ())),
                preferred_element_type=jnp.float32,
            )
            s = jnp.where(allowed, s * scale, NEG)
            top = jnp.max(s, axis=1, keepdims=True)
            if state is not None:
                top = jnp.maximum(top, state[3 * g])
            w = jnp.exp2(s - top)
            total = jnp.sum(w, axis=1, keepdims=True)
            acc = jnp.dot(w.astype(jnp.bfloat16), values, preferred_element_type=jnp.float32)
            if state is not None:
                keep = jnp.exp2(state[3 * g] - top)
                total += state[3 * g + 1] * keep
                acc += state[3 * g + 2] * keep
            out += [top, total, acc]
        return tuple(out)

    state = block(
        own_ref[:, :HEAD_WIDTH], own_ref[:, HEAD_WIDTH:], chip * span, None, True
    )
    for distance in range(1, 9):
        ref = far_refs[(distance - 1) // 2]
        low = ((distance - 1) % 2) * span
        base = (chip - distance) * span
        needed = (chip >= distance) & (base + span > first_start)
        state = lax.cond(
            needed,
            lambda st, ref=ref, low=low, base=base: block(
                ref[low : low + span, :HEAD_WIDTH],
                ref[low : low + span, HEAD_WIDTH:],
                base,
                st,
                False,
            ),
            lambda st: st,
            state,
        )
    for g in range(groups):
        lanes = slice(g * HEAD_WIDTH, (g + 1) * HEAD_WIDTH)
        out = (state[3 * g + 2] / state[3 * g + 1]).astype(jnp.bfloat16)
        first_ref[:, lanes] = out[:half]
        second_ref[:, lanes] = out[half:]


def local(queries, keys, values, row_route, lengths):
    n = lax.axis_size("ctx")
    index = lax.axis_index("ctx")
    tok, width = queries.shape
    groups = width // HEAD_WIDTH
    rows = n * SLOTS
    params = pltpu.CompilerParams(vmem_limit_bytes=48 * 2**20)
    bf16 = jnp.bfloat16

    packed_kv, pick = pl.pallas_call(
        functools.partial(pack_kernel, n),
        out_shape=(
            jax.ShapeDtypeStruct((rows, 2 * HEAD_WIDTH), bf16),
            jax.ShapeDtypeStruct((rows, tok), bf16),
        ),
        in_specs=[VMEM] * 3,
        out_specs=(VMEM, VMEM),
        compiler_params=params,
        name="pack",
    )(row_route.reshape(1, tok), keys, values)
    got_kv = lax.all_to_all(packed_kv.reshape(n, SLOTS, 2 * HEAD_WIDTH), "ctx", 0, 0, tiled=True)
    packed_q = jnp.dot(pick, queries, preferred_element_type=jnp.float32).astype(bf16)
    got_q = lax.all_to_all(packed_q.reshape(n, SLOTS, width), "ctx", 0, 0, tiled=True)

    my_kv, my_pick = pl.pallas_call(
        functools.partial(unpack_kernel, n),
        out_shape=(
            jax.ShapeDtypeStruct((tok, 2 * HEAD_WIDTH), bf16),
            jax.ShapeDtypeStruct((tok, rows), bf16),
        ),
        in_specs=[VMEM],
        out_specs=(VMEM, VMEM),
        compiler_params=params,
        name="unpack",
    )(got_kv.reshape(rows, 2 * HEAD_WIDTH))

    pairs = [[2 * c, 2 * c + 1] for c in range(n // 2)]

    def both_cores(x):
        return lax.all_gather(x, "ctx", axis_index_groups=pairs, axis=0, tiled=True)

    own = both_cores(my_kv)
    far = []
    for t in range(4):
        route = [
            (2 * (chip - 2 * t - 1 - core) + core, 2 * chip + core)
            for chip in range(n // 2)
            for core in range(2)
            if chip - 2 * t - 1 - core >= 0
        ]
        far.append(both_cores(lax.ppermute(own, "ctx", route)))

    first, second = pl.pallas_call(
        functools.partial(attend_kernel, groups),
        out_shape=(
            jax.ShapeDtypeStruct((tok // 2, width), bf16),
            jax.ShapeDtypeStruct((tok // 2, width), bf16),
        ),
        in_specs=[SMEM, SMEM] + [VMEM] * 7,
        out_specs=(VMEM, VMEM),
        scratch_shapes=[pltpu.VMEM((groups * tok, HEAD_WIDTH), bf16)],
        compiler_params=params,
        name="attend",
    )(lengths, index.astype(jnp.int32).reshape(1), my_pick, got_q.reshape(rows, width), own, *far)

    h = n // 2
    first = lax.ppermute(first, "ctx", [(j, 2 * j if j < h else 2 * n - 1 - 2 * j) for j in range(n)])
    second = lax.ppermute(
        second, "ctx", [(j, 2 * j + 1 if j < h else 2 * n - 2 - 2 * j) for j in range(n)]
    )
    even = index % 2 == 0
    return jnp.concatenate(
        [jnp.where(even, first, second), jnp.where(even, second, first)], axis=0
    )


def solution(mesh):
    placed = (P("ctx", "tp"), P("ctx", "tp"), P("ctx", "tp"), P("ctx"), P())
    return jax.shard_map(
        local, mesh=mesh, in_specs=placed, out_specs=P("ctx", "tp"), check_vma=False
    )
```

time: 256 us -> 132 us (0.52)
  the two profiles are of different devices: /device:TPU:1 before, /device:TPU:134 now
where the time goes in v1:
time: 132 us; the launch traced here: 131 us
  waiting for transfers between devices  49.4 us (37%)
  starting transfers between devices  44.3 us (34%)
  Pallas kernels  16.5 us (12%)
  blocking collectives  16.3 us (12%)
  local copies, waits for them, and re-layouts  2.32 us (2%)
  matrix products  1.41 us (1%)
    ppermute x4, waiting for transfers between devices, local(): far.append(both_cores(lax.ppermute(own, 'ctx', route)))  19.6 us
    ppermute x4, starting transfers between devices, local(): far.append(both_cores(lax.ppermute(own, 'ctx', route)))  19.1 us
    all_to_all x1, waiting for transfers between devices, local(): lax.all_to_all(packed_kv.reshape(n, SLOTS, 2 * HEAD_WIDTH), 'ctx', 0, 0,...  18.3 us
    all_gather x5, blocking collectives, both_cores(): return lax.all_gather(x, 'ctx', axis_index_groups=pairs, axis=0, tiled=True)  16.3 us
    all_to_all x1, starting transfers between devices, local(): lax.all_to_all(packed_kv.reshape(n, SLOTS, 2 * HEAD_WIDTH), 'ctx', 0, 0,...  14.9 us
    pallas_call x1, Pallas kernels, local(): pl.pallas_call(functools.partial(attend_kernel, groups), out_shape=(jax.S...  14.3 us
    ppermute x1, waiting for transfers between devices, local(): lax.ppermute(second, 'ctx', [(j, 2 * j + 1 if j < h else 2 * n - 2 - 2 *...  8.61 us
    all_to_all x1, starting transfers between devices, local(): lax.all_to_all(packed_q.reshape(n, SLOTS, width), 'ctx', 0, 0, tiled=True)  6.51 us
  transfers between devices with their start and end apart: 8, of which 4 were waited for; matrix products, arithmetic and copies ran while one was open for 1% of the time, Pallas kernels for 0%

profile of v1, /device:TPU:134, one launch (start us, length us, event | category | flops | bytes accessed | tf_op | source)
XLA Modules:
  0.0 131.1 jit_solution(13198298623548769855)
XLA Ops:
  0.0 0.0 copy-start
  0.0 0.0 copy-start.1
  0.0 0.8 copy-done.1
  0.8 0.0 copy-start.2
  0.8 0.8 copy-done.2
  1.6 0.0 copy-start.3
  1.6 0.7 copy-done.3
  2.3 1.6 %pack.1 = (bf16[1024,256]{1,0:T(8,128)(2,1)}, bf16[1024,192]{1,0:T(8,128)(2,1)S(1)}) custom-call(s32[1,192]{1,0:T(1,128)S(1)} %bitcast.10, bf16[192,128]{1,0:T(8,128)(2,1)S(1)} %copy-done.1, bf16[192,128]{1,0:T(8,128)(2,1)S(1)} %copy-done.2), custom_call_target="tpu_custom_call" | custom-call | tf_op jit(solution)/shard_map/pack/pallas_call | solution.py:184
  3.9 14.9 %all-to-all-start = ((bf16[64,16,256]{2,1,0:T(8,128)(2,1)}), bf16[64,16,256]{2,1,0:T(8,128)(2,1)S(1)}, u32[]{:S(2)}, u32[]{:S(2)}) async-start(bf16[64,16,256]{2,1,0:T(8,128)(2,1)} %bitcast.2), calls=%async_computation | async-start | bytes 1048576 | tf_op jit(solution)/shard_map/all_to_all | solution.py:195
  18.8 0.0 copy-done
  18.8 1.4 %convolution_convert_fusion = bf16[1024,512]{1,0:T(8,128)(2,1)} fusion(bf16[1024,192]{1,0:T(8,128)(2,1)S(1)} %get-tuple-element.13, bf16[192,512]{1,0:T(8,128)(2,1)S(1)} %copy-done), kind=kOutput, calls=%fused_computation | convolution fusion | flops 201850880 | bytes 1638400 | tf_op jit(solution)/shard_map/dot_general | solution.py:196
  20.2 18.3 %all-to-all-done = bf16[64,16,256]{2,1,0:T(8,128)(2,1)S(1)} async-done(((bf16[64,16,256]{2,1,0:T(8,128)(2,1)}), bf16[64,16,256]{2,1,0:T(8,128)(2,1)S(1)}, u32[]{:S(2)}, u32[]{:S(2)}) %all-to-all-start) | async-done | bytes 524320 | tf_op jit(solution)/shard_map/all_to_all | solution.py:195
  38.5 6.5 %all-to-all-start.1 = ((bf16[64,16,512]{2,1,0:T(8,128)(2,1)}), bf16[64,16,512]{2,1,0:T(8,128)(2,1)S(1)}, u32[]{:S(2)}, u32[]{:S(2)}) async-start(bf16[64,16,512]{2,1,0:T(8,128)(2,1)} %bitcast.4), calls=%async_computation.1 | async-start | bytes 2097152 | tf_op jit(solution)/shard_map/all_to_all | solution.py:197
  45.0 0.6 unpack.1
  45.6 1.9 %all_gather.15.own_ref = bf16[384,256]{1,0:T(8,128)(2,1)S(1)} all-gather(bf16[192,256]{1,0:T(8,128)(2,1)S(1)} %get-tuple-element.14), channel_id=1, replica_groups={{0,8},{16,24},{32,40},{48,56},{64,72},{80,88},{96,104},{112,120},{128,1..., dimensions={0}, use_global_device_ids=true | all-gather | bytes 294912 | tf_op jit(solution)/shard_map/all_gather | solution.py:214
  47.6 4.3 %collective-permute-start = (bf16[384,256]{1,0:T(8,128)(2,1)S(1)}, bf16[384,256]{1,0:T(8,128)(2,1)S(1)}, u32[]{:S(2)}, u32[]{:S(2)}) collective-permute-start(bf16[384,256]{1,0:T(8,128)(2,1)S(1)} %all_gather.15.own_ref), channel_id=1, source_target_pairs={{0,16},{16,32},{8,40},{32,48},{24,56},{48,64},{40,72},{64,80},{56,... | collective-permute-start | bytes 589832 | tf_op jit(solution)/shard_map/ppermute | solution.py:225
  51.8 4.6 %collective-permute-start.1 = (bf16[384,256]{1,0:T(8,128)(2,1)S(1)}, bf16[384,256]{1,0:T(8,128)(2,1)S(1)}, u32[]{:S(2)}, u32[]{:S(2)}) collective-permute-start(bf16[384,256]{1,0:T(8,128)(2,1)S(1)} %all_gather.15.own_ref), channel_id=1, source_target_pairs={{0,48},{16,64},{8,72},{32,80},{24,88},{48,96},{40,104},{64,112},{5... | collective-permute-start | bytes 589832 | tf_op jit(solution)/shard_map/ppermute | solution.py:225
  56.5 0.0 copy-start.4
  56.5 5.2 %collective-permute-start.2 = (bf16[384,256]{1,0:T(8,128)(2,1)S(1)}, bf16[384,256]{1,0:T(8,128)(2,1)S(1)}, u32[]{:S(2)}, u32[]{:S(2)}) collective-permute-start(bf16[384,256]{1,0:T(8,128)(2,1)S(1)} %all_gather.15.own_ref), channel_id=1, source_target_pairs={{0,80},{16,96},{8,104},{32,112},{24,120},{48,128},{40,136},{64,144... | collective-permute-start | bytes 589832 | tf_op jit(solution)/shard_map/ppermute | solution.py:225
  61.7 5.0 %collective-permute-start.3 = (bf16[384,256]{1,0:T(8,128)(2,1)S(1)}, bf16[384,256]{1,0:T(8,128)(2,1)S(1)}, u32[]{:S(2)}, u32[]{:S(2)}) collective-permute-start(bf16[384,256]{1,0:T(8,128)(2,1)S(1)} %all_gather.15.own_ref), channel_id=1, source_target_pairs={{0,112},{16,128},{8,136},{32,144},{24,152},{48,160},{40,168},{64,1... | collective-permute-start | bytes 589832 | tf_op jit(solution)/shard_map/ppermute | solution.py:225
  66.7 19.5 %collective-permute-done = bf16[384,256]{1,0:T(8,128)(2,1)S(1)} collective-permute-done((bf16[384,256]{1,0:T(8,128)(2,1)S(1)}, bf16[384,256]{1,0:T(8,128)(2,1)S(1)}, u32[]{:S(2)}, u32[]{:S(2)}) %collective-permute-start) | collective-permute-done | bytes 196640 | tf_op jit(solution)/shard_map/ppermute | solution.py:225
  86.3 2.1 %all_gather.16.rest_0_ = bf16[768,256]{1,0:T(8,128)(2,1)S(1)} all-gather(bf16[384,256]{1,0:T(8,128)(2,1)S(1)} %collective-permute-done), channel_id=1, replica_groups={{0,8},{16,24},{32,40},{48,56},{64,72},{80,88},{96,104},{112,120},{128,1..., dimensions={0}, use_global_device_ids=true | all-gather | bytes 589824 | tf_op jit(solution)/shard_map/all_gather | solution.py:214
  88.3 0.0 collective-permute-done.1
  88.3 8.1 %all_gather.17.rest_1_ = bf16[768,256]{1,0:T(8,128)(2,1)S(1)} all-gather(bf16[384,256]{1,0:T(8,128)(2,1)S(1)} %collective-permute-done.1), channel_id=1, replica_groups={{0,8},{16,24},{32,40},{48,56},{64,72},{80,88},{96,104},{112,120},{128,1..., dimensions={0}, use_global_device_ids=true | all-gather | bytes 589824 | tf_op jit(solution)/shard_map/all_gather | solution.py:214
  96.5 0.0 collective-permute-done.2
  96.5 2.1 %all_gather.18.rest_2_ = bf16[768,256]{1,0:T(8,128)(2,1)S(1)} all-gather(bf16[384,256]{1,0:T(8,128)(2,1)S(1)} %collective-permute-done.2), channel_id=1, replica_groups={{0,8},{16,24},{32,40},{48,56},{64,72},{80,88},{96,104},{112,120},{128,1..., dimensions={0}, use_global_device_ids=true | all-gather | bytes 589824 | tf_op jit(solution)/shard_map/all_gather | solution.py:214
  98.6 0.0 collective-permute-done.3
  98.6 2.1 %all_gather.19.rest_3_ = bf16[768,256]{1,0:T(8,128)(2,1)S(1)} all-gather(bf16[384,256]{1,0:T(8,128)(2,1)S(1)} %collective-permute-done.3), channel_id=1, replica_groups={{0,8},{16,24},{32,40},{48,56},{64,72},{80,88},{96,104},{112,120},{128,1..., dimensions={0}, use_global_device_ids=true | all-gather | bytes 589824 | tf_op jit(solution)/shard_map/all_gather | solution.py:214
  100.7 0.0 all-to-all-done.1
  100.7 0.0 copy-done.4
  100.7 14.3 %attend.1 = (bf16[96,512]{1,0:T(8,128)(2,1)}, bf16[96,512]{1,0:T(8,128)(2,1)S(1)}) custom-call(s32[16]{0:T(128)S(1)} %copy-done.4, s32[1]{0:T(128)} %bitcast.index_ref, bf16[192,1024]{1,0:T(8,128)(2,1)S(1)} %get-tuple-element.12.pick_ref, bf16[1024,512]{1,0:T(8,128)(2,1)S(1)} %bitcast.8, bf16[384,256]{1,0:T(8,128)(2,1)S(1)} %all_gather.15.own_ref, ...), custom_call_target="tpu_custom_call" | custom-call | tf_op jit(solution)/shard_map/attend/pallas_call | solution.py:227
  114.9 1.9 %collective-permute-start.4 = (bf16[96,512]{1,0:T(8,128)(2,1)}, bf16[96,512]{1,0:T(8,128)(2,1)S(1)}, u32[]{:S(2)}, u32[]{:S(2)}) collective-permute-start(bf16[96,512]{1,0:T(8,128)(2,1)} %get-tuple-element.15), channel_id=1, source_target_pairs={{0,0},{8,16},{16,32},{24,48},{32,64},{40,80},{48,96},{56,112},{64,... | collective-permute-start | bytes 294920 | tf_op jit(solution)/shard_map/ppermute | solution.py:241
  116.9 1.9 %collective-permute-start.5 = (bf16[96,512]{1,0:T(8,128)(2,1)S(1)}, bf16[96,512]{1,0:T(8,128)(2,1)S(1)}, u32[]{:S(2)}, u32[]{:S(2)}) collective-permute-start(bf16[96,512]{1,0:T(8,128)(2,1)S(1)} %get-tuple-element.16), channel_id=1, source_target_pairs={{0,8},{8,24},{16,40},{24,56},{32,72},{40,88},{48,104},{56,120},{64... | collective-permute-start | bytes 294920 | tf_op jit(solution)/shard_map/ppermute | solution.py:242
  118.8 2.9 %collective-permute-done.4 = bf16[96,512]{1,0:T(8,128)(2,1)S(1)} collective-permute-done((bf16[96,512]{1,0:T(8,128)(2,1)}, bf16[96,512]{1,0:T(8,128)(2,1)S(1)}, u32[]{:S(2)}, u32[]{:S(2)}) %collective-permute-start.4) | collective-permute-done | bytes 98336 | tf_op jit(solution)/shard_map/ppermute | solution.py:241
  121.7 8.6 %collective-permute-done.5 = bf16[96,512]{1,0:T(8,128)(2,1)S(1)} collective-permute-done((bf16[96,512]{1,0:T(8,128)(2,1)S(1)}, bf16[96,512]{1,0:T(8,128)(2,1)S(1)}, u32[]{:S(2)}, u32[]{:S(2)}) %collective-permute-start.5) | collective-permute-done | bytes 98336 | tf_op jit(solution)/shard_map/ppermute | solution.py:242
  130.4 0.7 pad_maximum_fusion
  (1 shorter events, 0.0 us)
Async XLA Ops:
  0.0 18.8 %copy-start = (bf16[192,512]{1,0:T(8,128)(2,1)S(1)}, bf16[192,512]{1,0:T(8,128)(2,1)}, u32[]{:S(2)}) copy-start(bf16[192,512]{1,0:T(8,128)(2,1)} %param.5) | copy-start | bytes 589828
  0.0 0.8 copy-start.1
  0.8 0.8 copy-start.2
  1.6 0.7 copy-start.3
  3.9 34.6 %all-to-all-start = ((bf16[64,16,256]{2,1,0:T(8,128)(2,1)}), bf16[64,16,256]{2,1,0:T(8,128)(2,1)S(1)}, u32[]{:S(2)}, u32[]{:S(2)}) async-start(bf16[64,16,256]{2,1,0:T(8,128)(2,1)} %bitcast.2), calls=%async_computation | async-start | bytes 1048576 | tf_op jit(solution)/shard_map/all_to_all | solution.py:195
  38.5 62.1 %all-to-all-start.1 = ((bf16[64,16,512]{2,1,0:T(8,128)(2,1)}), bf16[64,16,512]{2,1,0:T(8,128)(2,1)S(1)}, u32[]{:S(2)}, u32[]{:S(2)}) async-start(bf16[64,16,512]{2,1,0:T(8,128)(2,1)} %bitcast.4), calls=%async_computation.1 | async-start | bytes 2097152 | tf_op jit(solution)/shard_map/all_to_all | solution.py:197
  47.6 38.7 %collective-permute-start = (bf16[384,256]{1,0:T(8,128)(2,1)S(1)}, bf16[384,256]{1,0:T(8,128)(2,1)S(1)}, u32[]{:S(2)}, u32[]{:S(2)}) collective-permute-start(bf16[384,256]{1,0:T(8,128)(2,1)S(1)} %all_gather.15.own_ref), channel_id=1, source_target_pairs={{0,16},{16,32},{8,40},{32,48},{24,56},{48,64},{40,72},{64,80},{56,... | collective-permute-start | bytes 589832 | tf_op jit(solution)/shard_map/ppermute | solution.py:225
  51.8 36.5 %collective-permute-start.1 = (bf16[384,256]{1,0:T(8,128)(2,1)S(1)}, bf16[384,256]{1,0:T(8,128)(2,1)S(1)}, u32[]{:S(2)}, u32[]{:S(2)}) collective-permute-start(bf16[384,256]{1,0:T(8,128)(2,1)S(1)} %all_gather.15.own_ref), channel_id=1, source_target_pairs={{0,48},{16,64},{8,72},{32,80},{24,88},{48,96},{40,104},{64,112},{5... | collective-permute-start | bytes 589832 | tf_op jit(solution)/shard_map/ppermute | solution.py:225
  56.5 44.2 %copy-start.4 = (s32[16]{0:T(128)S(1)}, s32[16]{0:T(128)}, u32[]{:S(2)}) copy-start(s32[16]{0:T(128)} %lengths_ref.1) | copy-start | bytes 196
  56.5 40.0 %collective-permute-start.2 = (bf16[384,256]{1,0:T(8,128)(2,1)S(1)}, bf16[384,256]{1,0:T(8,128)(2,1)S(1)}, u32[]{:S(2)}, u32[]{:S(2)}) collective-permute-start(bf16[384,256]{1,0:T(8,128)(2,1)S(1)} %all_gather.15.own_ref), channel_id=1, source_target_pairs={{0,80},{16,96},{8,104},{32,112},{24,120},{48,128},{40,136},{64,144... | collective-permute-start | bytes 589832 | tf_op jit(solution)/shard_map/ppermute | solution.py:225
  61.7 36.8 %collective-permute-start.3 = (bf16[384,256]{1,0:T(8,128)(2,1)S(1)}, bf16[384,256]{1,0:T(8,128)(2,1)S(1)}, u32[]{:S(2)}, u32[]{:S(2)}) collective-permute-start(bf16[384,256]{1,0:T(8,128)(2,1)S(1)} %all_gather.15.own_ref), channel_id=1, source_target_pairs={{0,112},{16,128},{8,136},{32,144},{24,152},{48,160},{40,168},{64,1... | collective-permute-start | bytes 589832 | tf_op jit(solution)/shard_map/ppermute | solution.py:225
  114.9 6.8 %collective-permute-start.4 = (bf16[96,512]{1,0:T(8,128)(2,1)}, bf16[96,512]{1,0:T(8,128)(2,1)S(1)}, u32[]{:S(2)}, u32[]{:S(2)}) collective-permute-start(bf16[96,512]{1,0:T(8,128)(2,1)} %get-tuple-element.15), channel_id=1, source_target_pairs={{0,0},{8,16},{16,32},{24,48},{32,64},{40,80},{48,96},{56,112},{64,... | collective-permute-start | bytes 294920 | tf_op jit(solution)/shard_map/ppermute | solution.py:241
  116.9 13.5 %collective-permute-start.5 = (bf16[96,512]{1,0:T(8,128)(2,1)S(1)}, bf16[96,512]{1,0:T(8,128)(2,1)S(1)}, u32[]{:S(2)}, u32[]{:S(2)}) collective-permute-start(bf16[96,512]{1,0:T(8,128)(2,1)S(1)} %get-tuple-element.16), channel_id=1, source_target_pairs={{0,8},{8,24},{16,40},{24,56},{32,72},{40,88},{48,104},{56,120},{64... | collective-permute-start | bytes 294920 | tf_op jit(solution)/shard_map/ppermute | solution.py:242

commit v2 on v0

v2 whole, which is shorter than its diff:
```python
import functools
import math

import jax
import jax.numpy as jnp
from jax import lax
from jax.experimental import pallas as pl
from jax.experimental.pallas import tpu as pltpu
from jax.sharding import PartitionSpec as P

HEAD_WIDTH = 128
SLOTS = 8
CAP = 6
PLANE = 8
STEPS = 4
NEG = -1e30
VMEM = pl.BlockSpec(memory_space=pltpu.VMEM)
ANY = pl.BlockSpec(memory_space=pl.ANY)
SMEM = pl.BlockSpec(memory_space=pltpu.SMEM)


def iota(shape, dim):
    return lax.broadcasted_iota(jnp.int32, shape, dim)


def divide(x, by):
    return ((x.astype(jnp.float32) + 0.5) * (1.0 / by)).astype(jnp.int32)


def hot(mask):
    return jnp.where(mask, jnp.float32(1), jnp.float32(0)).astype(jnp.bfloat16)


def times(a, b):
    return jnp.dot(a, b, preferred_element_type=jnp.float32)


def times_t(a, b):
    return lax.dot_general(a, b, (((1,), (1,)), ((), ())), preferred_element_type=jnp.float32)


def pack_kernel(n, route_hbm, q_hbm, k_hbm, v_hbm, out_ref, route_ref, q_ref, k_ref, v_ref, sems):
    copies = [
        pltpu.make_async_copy(src, dst, sems.at[i])
        for i, (src, dst) in enumerate(
            ((route_hbm, route_ref), (k_hbm, k_ref), (v_hbm, v_ref), (q_hbm, q_ref))
        )
    ]
    for copy in copies:
        copy.start()
    tok, width = q_ref.shape
    rows = n * SLOTS
    copies[0].wait()
    route = route_ref[...]
    owner = divide(route, tok)
    slot = route - owner * tok
    square = (tok, tok)
    down, across = iota(square, 0), iota(square, 1)
    along = jnp.broadcast_to(owner, square)
    column = jnp.sum(jnp.where(down == across, along, 0), axis=1, keepdims=True)
    order = jnp.sum(
        jnp.where((column == along) & (down < across), 1, 0), axis=0, keepdims=True
    )
    wide = (rows, tok)
    line = iota(wide, 0)
    to = owner * SLOTS

    def pick(row, valid=None):
        where_to = to + row
        if valid is not None:
            where_to = jnp.where(valid, where_to, -1)
        return hot(line == jnp.broadcast_to(where_to, wide))

    value_picks = {
        group: pick(CAP + order - first, (order >= first) & (order < first + 2))
        for group, first in ((4, 0), (0, 2), (1, 4))
    }
    lanes = (HEAD_WIDTH, tok)
    places = jnp.where(
        iota(lanes, 0) == jnp.broadcast_to(order, lanes),
        jnp.broadcast_to(slot + 1, lanes).astype(jnp.float32),
        jnp.float32(0),
    ).astype(jnp.bfloat16)
    extra = {2: times_t(pick(CAP), places)}
    main = pick(order)
    copies[1].wait()
    copies[2].wait()
    for group, chosen in value_picks.items():
        extra[group] = times(chosen, v_ref[...])
    extra[4] += times(main, k_ref[...])
    copies[3].wait()
    packed = times(main, q_ref[...])
    for group in range(5):
        part = slice(group * HEAD_WIDTH, (group + 1) * HEAD_WIDTH)
        value = extra.get(group)
        if group < 4:
            value = packed[:, part] if value is None else packed[:, part] + value
        out_ref[:, part] = value.astype(jnp.bfloat16)


def unpack_kernel(n, keys, index_ref, got_ref, *outs):
    rows = n * SLOTS
    tall = (n, rows)
    mark_row = iota(tall, 0) * SLOTS + CAP

    def group(i):
        return got_ref[:, i * HEAD_WIDTH : (i + 1) * HEAD_WIDTH]

    marks = times(hot(iota(tall, 1) == mark_row), group(2)).astype(jnp.bfloat16)
    mine = iota(tall, 1) - iota(tall, 0) * SLOTS
    mine = (mine >= 0) & (mine < SLOTS)
    lanes = (HEAD_WIDTH, rows)
    row = iota(lanes, 1) & (SLOTS - 1)

    def place_of(lane):
        spread = times(marks, hot(iota(lanes, 0) == lane))
        return jnp.sum(jnp.where(mine, spread, jnp.float32(0)), axis=0, keepdims=True)

    def pick(place, count, offset):
        wide = (count, rows)
        want = (iota(wide, 0) + 1 + offset).astype(jnp.float32)
        return hot(want == jnp.broadcast_to(place, wide))

    main = place_of(jnp.where(row < CAP, row, -1))
    if keys:
        (kv_ref,) = outs
        tok = kv_ref.shape[0]
        kv_ref[:, :HEAD_WIDTH] = times(pick(main, tok, 0), group(4)).astype(jnp.bfloat16)
        v = sum(
            times(pick(place_of(jnp.where(row >= CAP, row - CAP + first, -1)), tok, 0), group(at))
            for at, first in ((4, 0), (0, 2), (1, 4))
        )
        kv_ref[:, HEAD_WIDTH:] = v.astype(jnp.bfloat16)
        return
    half, width = outs[0].shape
    even = index_ref[0] % 2 == 0
    for ref, own in zip(outs, (even, jnp.logical_not(even))):
        chosen = pick(main, half, jnp.where(own, 0, half))
        ref[...] = times(chosen, got_ref[:, :width]).astype(jnp.bfloat16)


def attend_kernel(n, groups, lengths_ref, index_ref, q1_ref, q2_ref, *rest):
    key_refs, value_refs = rest[:STEPS], rest[STEPS : 2 * STEPS]
    heads_ref, top_ref, acc_ref, scores_ref = rest[2 * STEPS :]
    half = q1_ref.shape[0]
    tok = 2 * half
    span = key_refs[0].shape[0]
    index = index_ref[0]
    even = index % 2 == 0
    chunk = jnp.where(even, index // 2, n - 1 - index // 2)
    first_row = chunk * tok
    run = first_row // span
    scale = HEAD_WIDTH ** (-0.5) * math.log2(math.e)

    for g in range(groups):
        lanes = slice(g * HEAD_WIDTH, (g + 1) * HEAD_WIDTH)
        for ref, at in ((q1_ref, g * tok), (q2_ref, g * tok + half)):
            scaled = ref[:, lanes].astype(jnp.float32) * scale
            upper = scaled.astype(jnp.bfloat16)
            lower = (scaled - upper.astype(jnp.float32)).astype(jnp.bfloat16)
            heads_ref[at : at + half, :HEAD_WIDTH] = upper
            heads_ref[at : at + half, HEAD_WIDTH:] = lower

    column = (tok, HEAD_WIDTH)
    query_pos = first_row + iota(column, 0)
    start = jnp.zeros(column, jnp.int32)
    first_start = last_start = end = jnp.int32(0)
    for i in range(lengths_ref.shape[0]):
        end = end + lengths_ref[i]
        start = jnp.where(query_pos >= end, end, start)
        first_start = jnp.where(first_row >= end, end, first_start)
        last_start = jnp.where(first_row + tok - 1 >= end, end, last_start)

    def score(step, base, masked):
        k = key_refs[step][...]
        k = jnp.concatenate([k, k], axis=1)
        own = step == 0
        reach = span // HEAD_WIDTH
        if masked:
            key_pos = base + iota((tok, span), 1)
            allowed = key_pos >= jnp.concatenate([start] * reach, axis=1)
            if own:
                allowed &= key_pos <= jnp.concatenate([query_pos] * reach, axis=1)
        for g in range(groups):
            rows = slice(g * tok, (g + 1) * tok)
            s = times_t(heads_ref[rows, :], k)
            if masked:
                s = jnp.where(allowed, s, NEG)
            scores_ref[rows, step * span : (step + 1) * span] = s
            top = s[:, :HEAD_WIDTH]
            for i in range(1, reach):
                top = jnp.maximum(top, s[:, i * HEAD_WIDTH : (i + 1) * HEAD_WIDTH])
            if not own:
                top = jnp.maximum(top, top_ref[rows, :])
            top_ref[rows, :] = top

    def weigh(step):
        v = value_refs[step][...]
        v = jnp.concatenate([v, jnp.ones_like(v)], axis=1)
        for g in range(groups):
            rows = slice(g * tok, (g + 1) * tok)
            top = jnp.concatenate([top_ref[rows, :]] * (span // HEAD_WIDTH), axis=1)
            w = jnp.exp2(scores_ref[rows, step * span : (step + 1) * span] - top)
            acc = times(w.astype(jnp.bfloat16), v)
            if step:
                acc += acc_ref[rows, :]
            acc_ref[rows, :] = acc

    bases = [(run - step) * span for step in range(STEPS)]

    def needed(step):
        return (bases[step] >= 0) & (bases[step] + span > first_start)

    score(0, bases[0], True)
    for step in range(1, STEPS):
        clear = bases[step] >= last_start

        @pl.when(needed(step) & clear)
        def _(step=step):
            score(step, bases[step], False)

        @pl.when(needed(step) & jnp.logical_not(clear))
        def _(step=step):
            score(step, bases[step], True)

    for g in range(groups):
        rows = slice(g * tok, (g + 1) * tok)
        top = jnp.max(top_ref[rows, :], axis=1, keepdims=True)
        top_ref[rows, :] = jnp.broadcast_to(top, column)

    weigh(0)
    for step in range(1, STEPS):

        @pl.when(needed(step))
        def _(step=step):
            weigh(step)


def finish_kernel(
    n, groups, lengths_ref, index_ref, heads_ref, top_ref, acc_ref, key_ref, value_ref, first_ref, second_ref
):
    tok = heads_ref.shape[0] // groups
    half = tok // 2
    span = key_ref.shape[0]
    reach = span // HEAD_WIDTH
    index = index_ref[0]
    chunk = jnp.where(index % 2 == 0, index // 2, n - 1 - index // 2)
    first_row = chunk * tok
    base = (first_row // span - STEPS) * span
    column = (tok, HEAD_WIDTH)
    start = jnp.zeros(column, jnp.int32)
    first_start = end = jnp.int32(0)
    for i in range(lengths_ref.shape[0]):
        end = end + lengths_ref[i]
        start = jnp.where(first_row + iota(column, 0) >= end, end, start)
        first_start = jnp.where(first_row >= end, end, first_start)

    def write(g, acc):
        lanes = slice(g * HEAD_WIDTH, (g + 1) * HEAD_WIDTH)
        out = (acc[:, :HEAD_WIDTH] / acc[:, HEAD_WIDTH:]).astype(jnp.bfloat16)
        first_ref[:, lanes] = out[:half]
        second_ref[:, lanes] = out[half:]

    needed = (base >= 0) & (base + span > first_start)

    @pl.when(needed)
    def _():
        k, v = key_ref[...], value_ref[...]
        k = jnp.concatenate([k, k], axis=1)
        v = jnp.concatenate([v, jnp.ones_like(v)], axis=1)
        key_pos = base + iota((tok, span), 1)
        allowed = key_pos >= jnp.concatenate([start] * reach, axis=1)
        for g in range(groups):
            rows = slice(g * tok, (g + 1) * tok)
            s = jnp.where(allowed, times_t(heads_ref[rows, :], k), NEG)
            top = s[:, :HEAD_WIDTH]
            for i in range(1, reach):
                top = jnp.maximum(top, s[:, i * HEAD_WIDTH : (i + 1) * HEAD_WIDTH])
            top = jnp.broadcast_to(jnp.max(top, axis=1, keepdims=True), column)
            before = top_ref[rows, :]
            top = jnp.maximum(top, before)
            w = jnp.exp2(s - jnp.concatenate([top] * reach, axis=1)).astype(jnp.bfloat16)
            keep = jnp.exp2(before - top)
            write(g, times(w, v) + acc_ref[rows, :] * jnp.concatenate([keep, keep], axis=1))

    @pl.when(jnp.logical_not(needed))
    def _():
        for g in range(groups):
            write(g, acc_ref[g * tok : (g + 1) * tok, :])


def local(queries, keys, values, row_route, lengths):
    n = lax.axis_size("ctx")
    index = lax.axis_index("ctx")
    tok, width = queries.shape
    half = tok // 2
    groups = width // HEAD_WIDTH
    rows = n * SLOTS
    lanes = width + HEAD_WIDTH
    bf16 = jnp.bfloat16
    here = index.astype(jnp.int32).reshape(1)
    even = index % 2 == 0

    packed = pl.pallas_call(
        functools.partial(pack_kernel, n),
        out_shape=jax.ShapeDtypeStruct((rows, lanes), bf16),
        in_specs=[ANY] * 4,
        out_specs=VMEM,
        scratch_shapes=[
            pltpu.VMEM((1, tok), jnp.int32),
            pltpu.VMEM((tok, width), bf16),
            pltpu.VMEM((tok, HEAD_WIDTH), bf16),
            pltpu.VMEM((tok, HEAD_WIDTH), bf16),
            pltpu.SemaphoreType.DMA((4,)),
        ],
        compiler_params=pltpu.CompilerParams(vmem_limit_bytes=60 * 2**20),
        name="pack",
    )(row_route.reshape(1, tok), queries, keys, values)
    got = lax.all_to_all(packed.reshape(n, SLOTS, lanes), "ctx", 0, 0, tiled=True)

    params = pltpu.CompilerParams(vmem_limit_bytes=48 * 2**20)
    part = jax.ShapeDtypeStruct((half, width), bf16)
    got = got.reshape(rows, lanes)

    def unpack(keys, *shapes):
        return pl.pallas_call(
            functools.partial(unpack_kernel, n, keys),
            out_shape=shapes,
            in_specs=[SMEM, VMEM],
            out_specs=(VMEM,) * len(shapes),
            compiler_params=params,
            name="unpack_kv" if keys else "unpack_q",
        )(here, got)

    (my_kv,) = unpack(True, jax.ShapeDtypeStruct((tok, 2 * HEAD_WIDTH), bf16))
    keep, give = unpack(False, part, part)

    planes = n // PLANE
    groups_of = [list(range(z * PLANE, (z + 1) * PLANE)) for z in range(planes)]
    plane = lax.all_gather(my_kv, "ctx", axis_index_groups=groups_of, axis=0, tiled=True)
    plane = plane.reshape(PLANE, 2, half, 2 * HEAD_WIDTH)
    run = jnp.where(even, plane[:, 0], plane[::-1, 1]).reshape(PLANE * half, 2 * HEAD_WIDTH)
    run_keys, run_values = [run[:, :HEAD_WIDTH]], [run[:, HEAD_WIDTH:]]
    chain = []
    for chip in range(PLANE // 2):
        stops = [z * PLANE + 2 * chip for z in range(planes)]
        stops += [stop + 1 for stop in reversed(stops)]
        chain += list(zip(stops[:-1], stops[1:]))
    for step in range(STEPS):
        run_keys.append(lax.ppermute(run_keys[step], "ctx", chain))
        run_values.append(lax.ppermute(run_values[step], "ctx", chain))

    swap = [(i, i ^ 1) for i in range(n)]
    taken = lax.ppermute(give, "ctx", swap)
    sums = (
        jax.ShapeDtypeStruct((groups * tok, 2 * HEAD_WIDTH), bf16),
        jax.ShapeDtypeStruct((groups * tok, HEAD_WIDTH), jnp.float32),
        jax.ShapeDtypeStruct((groups * tok, 2 * HEAD_WIDTH), jnp.float32),
    )
    params = pltpu.CompilerParams(vmem_limit_bytes=32 * 2**20)
    pairs = groups * tok * PLANE * half
    state = pl.pallas_call(
        functools.partial(attend_kernel, n, groups),
        out_shape=sums,
        in_specs=[SMEM, SMEM] + [VMEM] * (2 * STEPS + 2),
        out_specs=(VMEM,) * 3,
        scratch_shapes=[pltpu.VMEM((groups * tok, STEPS * PLANE * half), jnp.float32)],
        compiler_params=params,
        cost_estimate=pl.CostEstimate(
            flops=64 * STEPS * HEAD_WIDTH * pairs,
            bytes_accessed=2**23,
            transcendentals=8 * STEPS * pairs,
        ),
        name="attend",
    )(lengths, here, keep, taken, *run_keys[:STEPS], *run_values[:STEPS])
    first, second = pl.pallas_call(
        functools.partial(finish_kernel, n, groups),
        out_shape=(part, part),
        in_specs=[SMEM, SMEM] + [VMEM] * 5,
        out_specs=(VMEM, VMEM),
        compiler_params=params,
        name="finish",
    )(lengths, here, *state, run_keys[STEPS], run_values[STEPS])

    second = lax.ppermute(second, "ctx", swap)
    return jnp.concatenate(
        [jnp.where(even, first, second), jnp.where(even, second, first)], axis=0
    )


def solution(mesh):
    placed = (P("ctx", "tp"), P("ctx", "tp"), P("ctx", "tp"), P("ctx"), P())
    return jax.shard_map(
        local, mesh=mesh, in_specs=placed, out_specs=P("ctx", "tp"), check_vma=False
    )
```

time: 256 us -> 101 us (0.39)
  waiting for transfers between devices: 134 us -> 37.3 us
  matrix products: 35.8 us -> 0 us
  other arithmetic: 22.9 us -> 0.81 us
  local copies, waits for them, and re-layouts: 17.4 us -> 0.06 us
  blocking collectives: 0 us -> 15.3 us
  between operations: 13.6 us -> 0.19 us
  starting transfers between devices: 31.4 us -> 39.5 us
  Pallas kernels: 0 us -> 7.2 us
    all_gather x2 -> x0, waiting for transfers between devices: 87.4 us -> none  [the longest x1 49.3 us: local(): lax.all_gather(local_values, 'ctx', axis=0, tiled=True)]
    dot_general x2 -> x0, matrix products: 35.8 us -> none  [the longest x1 18 us: local(): jnp.einsum('tkgd,skd->kgts', query_heads, heads_of_key, preferred_element...]
    all_to_all x4 -> x1, waiting for transfers between devices: 46.8 us -> 23.8 us  [local(): lax.all_to_all(packed.reshape(n, SLOTS, lanes), 'ctx', 0, 0, tiled=True)]
    ppermute x0 -> x10, starting transfers between devices: none -> 21.9 us  [the longest x1 7.21 us: local(): taken = lax.ppermute(give, 'ctx', swap)]
    reduce_sum x4 -> x0, other arithmetic: 18.5 us -> none  [the longest x1 18.1 us: local(): new_total = jnp.sum(weight, axis=3)]
    all_gather x0 -> x1, blocking collectives: none -> 15.3 us  [local(): lax.all_gather(my_kv, 'ctx', axis_index_groups=groups_of, axis=0, tiled=T...]
    all_to_all x4 -> x1, starting transfers between devices: 31.3 us -> 17.6 us  [local(): lax.all_to_all(packed.reshape(n, SLOTS, lanes), 'ctx', 0, 0, tiled=True)]
    ppermute x0 -> x10, waiting for transfers between devices: none -> 13.5 us  [the longest x4 8.7 us: local(): run_keys.append(lax.ppermute(run_keys[step], 'ctx', chain))]
  transfers between devices with their start and end apart: 6 -> 11, of which waited for: 6 -> 8; matrix products, arithmetic and copies ran while one was open for 19% -> 0% of each run, Pallas kernels for 0% -> 2%
where the time goes in v2:
time: 101 us; the launch traced here: 100 us
  starting transfers between devices  39.5 us (39%)
  waiting for transfers between devices  37.3 us (37%)
  blocking collectives  15.3 us (15%)
  Pallas kernels  7.2 us (7%)
    all_to_all x1, waiting for transfers between devices, local(): lax.all_to_all(packed.reshape(n, SLOTS, lanes), 'ctx', 0, 0, tiled=True)  23.8 us
    all_to_all x1, starting transfers between devices, local(): lax.all_to_all(packed.reshape(n, SLOTS, lanes), 'ctx', 0, 0, tiled=True)  17.6 us
    all_gather x1, blocking collectives, local(): lax.all_gather(my_kv, 'ctx', axis_index_groups=groups_of, axis=0, tiled=T...  15.3 us
    ppermute x4, waiting for transfers between devices, local(): run_keys.append(lax.ppermute(run_keys[step], 'ctx', chain))  8.7 us
    ppermute x1, starting transfers between devices, local(): taken = lax.ppermute(give, 'ctx', swap)  7.21 us
    ppermute x4, starting transfers between devices, local(): run_keys.append(lax.ppermute(run_keys[step], 'ctx', chain))  5.15 us
    ppermute x4, starting transfers between devices, local(): run_values.append(lax.ppermute(run_values[step], 'ctx', chain))  5.15 us
    ppermute x1, starting transfers between devices, local(): second = lax.ppermute(second, 'ctx', swap)  4.37 us
  transfers between devices with their start and end apart: 11, of which 8 were waited for; matrix products, arithmetic and copies ran while one was open for 0% of the time, Pallas kernels for 2%

profile of v2, /device:TPU:1, one launch (start us, length us, event | category | flops | bytes accessed | tf_op | source)
XLA Modules:
  0.0 100.4 jit_solution(11670675985250818754)
XLA Ops:
  0.0 3.0 %pack.1 = bf16[512,640]{1,0:T(8,128)(2,1)} custom-call(s32[1,192]{1,0:T(1,128)} %bitcast.18, bf16[192,512]{1,0:T(8,128)(2,1)} %q_hbm.1, bf16[192,128]{1,0:T(8,128)(2,1)} %k_hbm.1, bf16[192,128]{1,0:T(8,128)(2,1)} %v_hbm.1), custom_call_target="tpu_custom_call" | custom-call | tf_op jit(solution)/shard_map/pack/pallas_call | solution.py:304
  3.0 17.6 %all-to-all-start = ((bf16[64,8,640]{2,1,0:T(8,128)(2,1)}), bf16[64,8,640]{2,1,0:T(8,128)(2,1)S(1)}, u32[]{:S(2)}, u32[]{:S(2)}) async-start(bf16[64,8,640]{2,1,0:T(8,128)(2,1)} %bitcast.16), calls=%async_computation | async-start | bytes 1310720 | tf_op jit(solution)/shard_map/all_to_all | solution.py:319
  20.7 23.8 %all-to-all-done = bf16[64,8,640]{2,1,0:T(8,128)(2,1)S(1)} async-done(((bf16[64,8,640]{2,1,0:T(8,128)(2,1)}), bf16[64,8,640]{2,1,0:T(8,128)(2,1)S(1)}, u32[]{:S(2)}, u32[]{:S(2)}) %all-to-all-start) | async-done | bytes 655392 | tf_op jit(solution)/shard_map/all_to_all | solution.py:319
  44.5 1.0 unpack_kv.1
  45.5 15.3 %all_gather.3 = bf16[1536,256]{1,0:T(8,128)(2,1)S(1)} all-gather(bf16[192,256]{1,0:T(8,128)(2,1)S(1)} %unpack_kv.1), channel_id=1, replica_groups={{0,8,16,24,32,40,48,56},{64,72,80,88,96,104,112,120},{128,136,144,152,1..., dimensions={0}, use_global_device_ids=true | all-gather | bytes 884736 | tf_op jit(solution)/shard_map/all_gather | solution.py:340
  60.9 0.1 fusion
  61.0 1.3 %collective-permute-start.1 = (bf16[768,128]{1,0:T(8,128)(2,1)S(1)}, bf16[768,128]{1,0:T(8,128)(2,1)S(1)}, u32[]{:S(2)}, u32[]{:S(2)}) collective-permute-start(bf16[768,128]{1,0:T(8,128)(2,1)S(1)} %get-tuple-element.20.rest_0_), channel_id=1, source_target_pairs={{0,64},{64,128},{128,192},{192,256},{256,320},{320,384},{384,448},... | collective-permute-start | bytes 589832 | tf_op jit(solution)/shard_map/ppermute | solution.py:350
  62.3 1.3 %collective-permute-start.4 = (bf16[768,128]{1,0:T(8,128)(2,1)S(1)}, bf16[768,128]{1,0:T(8,128)(2,1)S(1)}, u32[]{:S(2)}, u32[]{:S(2)}) collective-permute-start(bf16[768,128]{1,0:T(8,128)(2,1)S(1)} %get-tuple-element.19.rest_4_), channel_id=1, source_target_pairs={{0,64},{64,128},{128,192},{192,256},{256,320},{320,384},{384,448},... | collective-permute-start | bytes 589832 | tf_op jit(solution)/shard_map/ppermute | solution.py:351
  63.6 3.8 %collective-permute-done.1.rest_1_ = bf16[768,128]{1,0:T(8,128)(2,1)S(1)} collective-permute-done((bf16[768,128]{1,0:T(8,128)(2,1)S(1)}, bf16[768,128]{1,0:T(8,128)(2,1)S(1)}, u32[]{:S(2)}, u32[]{:S(2)}) %collective-permute-start.1) | collective-permute-done | bytes 196640 | tf_op jit(solution)/shard_map/ppermute | solution.py:350
  67.4 1.3 %collective-permute-start.2 = (bf16[768,128]{1,0:T(8,128)(2,1)S(1)}, bf16[768,128]{1,0:T(8,128)(2,1)S(1)}, u32[]{:S(2)}, u32[]{:S(2)}) collective-permute-start(bf16[768,128]{1,0:T(8,128)(2,1)S(1)} %collective-permute-done.1.rest_1_), channel_id=1, source_target_pairs={{0,64},{64,128},{128,192},{192,256},{256,320},{320,384},{384,448},... | collective-permute-start | bytes 589832 | tf_op jit(solution)/shard_map/ppermute | solution.py:350
  68.7 0.8 collective-permute-done.4.rest_5_
  69.5 1.3 %collective-permute-start.5 = (bf16[768,128]{1,0:T(8,128)(2,1)S(1)}, bf16[768,128]{1,0:T(8,128)(2,1)S(1)}, u32[]{:S(2)}, u32[]{:S(2)}) collective-permute-start(bf16[768,128]{1,0:T(8,128)(2,1)S(1)} %collective-permute-done.4.rest_5_), channel_id=1, source_target_pairs={{0,64},{64,128},{128,192},{192,256},{256,320},{320,384},{384,448},... | collective-permute-start | bytes 589832 | tf_op jit(solution)/shard_map/ppermute | solution.py:351
  70.8 3.0 %collective-permute-done.2.rest_2_ = bf16[768,128]{1,0:T(8,128)(2,1)S(1)} collective-permute-done((bf16[768,128]{1,0:T(8,128)(2,1)S(1)}, bf16[768,128]{1,0:T(8,128)(2,1)S(1)}, u32[]{:S(2)}, u32[]{:S(2)}) %collective-permute-start.2) | collective-permute-done | bytes 196640 | tf_op jit(solution)/shard_map/ppermute | solution.py:350
  73.8 1.3 %collective-permute-start.3 = (bf16[768,128]{1,0:T(8,128)(2,1)S(1)}, bf16[768,128]{1,0:T(8,128)(2,1)S(1)}, u32[]{:S(2)}, u32[]{:S(2)}) collective-permute-start(bf16[768,128]{1,0:T(8,128)(2,1)S(1)} %collective-permute-done.2.rest_2_), channel_id=1, source_target_pairs={{0,64},{64,128},{128,192},{192,256},{256,320},{320,384},{384,448},... | collective-permute-start | bytes 589832 | tf_op jit(solution)/shard_map/ppermute | solution.py:350
  75.1 0.9 collective-permute-done.5.rest_6_
  76.0 1.3 %collective-permute-start.6 = (bf16[768,128]{1,0:T(8,128)(2,1)S(1)}, bf16[768,128]{1,0:T(8,128)(2,1)S(1)}, u32[]{:S(2)}, u32[]{:S(2)}) collective-permute-start(bf16[768,128]{1,0:T(8,128)(2,1)S(1)} %collective-permute-done.5.rest_6_), channel_id=1, source_target_pairs={{0,64},{64,128},{128,192},{192,256},{256,320},{320,384},{384,448},... | collective-permute-start | bytes 589832 | tf_op jit(solution)/shard_map/ppermute | solution.py:351
  77.3 0.6 unpack_q.1
  77.9 0.0 copy-start
  77.9 7.2 %collective-permute-start = (bf16[96,512]{1,0:T(8,128)(2,1)S(1)}, bf16[96,512]{1,0:T(8,128)(2,1)S(1)}, u32[]{:S(2)}, u32[]{:S(2)}) collective-permute-start(bf16[96,512]{1,0:T(8,128)(2,1)S(1)} %get-tuple-element.13), channel_id=1, source_target_pairs={{0,8},{8,0},{16,24},{24,16},{32,40},{40,32},{48,56},{56,48},{64,72... | collective-permute-start | bytes 294920 | tf_op jit(solution)/shard_map/ppermute | solution.py:354
  85.1 0.0 collective-permute-done.3.rest_3_
  85.1 1.3 %collective-permute-start.7 = (bf16[768,128]{1,0:T(8,128)(2,1)S(1)}, bf16[768,128]{1,0:T(8,128)(2,1)S(1)}, u32[]{:S(2)}, u32[]{:S(2)}) collective-permute-start(bf16[768,128]{1,0:T(8,128)(2,1)S(1)} %collective-permute-done.3.rest_3_), channel_id=1, source_target_pairs={{0,64},{64,128},{128,192},{192,256},{256,320},{320,384},{384,448},... | collective-permute-start | bytes 589832 | tf_op jit(solution)/shard_map/ppermute | solution.py:350
  86.4 0.0 collective-permute-done.6.rest_7_
  86.5 1.3 %collective-permute-start.8 = (bf16[768,128]{1,0:T(8,128)(2,1)S(1)}, bf16[768,128]{1,0:T(8,128)(2,1)S(1)}, u32[]{:S(2)}, u32[]{:S(2)}) collective-permute-start(bf16[768,128]{1,0:T(8,128)(2,1)S(1)} %collective-permute-done.6.rest_7_), channel_id=1, source_target_pairs={{0,64},{64,128},{128,192},{192,256},{256,320},{320,384},{384,448},... | collective-permute-start | bytes 589832 | tf_op jit(solution)/shard_map/ppermute | solution.py:351
  87.8 0.0 collective-permute-done.q2_ref
  87.8 0.0 copy-done
  87.8 1.9 %attend.1 = (bf16[768,256]{1,0:T(8,128)(2,1)S(1)}, f32[768,128]{1,0:T(8,128)S(1)}, f32[768,256]{1,0:T(8,128)S(1)}) custom-call(s32[16]{0:T(128)S(1)} %copy-done, s32[1]{0:T(128)} %bitcast.index_ref, bf16[96,512]{1,0:T(8,128)(2,1)S(1)} %get-tuple-element.12.q1_ref, bf16[96,512]{1,0:T(8,128)(2,1)S(1)} %collective-permute-done.q2_ref, ...), custom_call_target="tpu_custom_call" | custom-call | flops 19327352832 | bytes 8388608 | tf_op jit(solution)/shard_map/attend/pallas_call | solution.py:362
  89.7 1.9 %collective-permute-done.7.key_ref = bf16[768,128]{1,0:T(8,128)(2,1)S(1)} collective-permute-done((bf16[768,128]{1,0:T(8,128)(2,1)S(1)}, bf16[768,128]{1,0:T(8,128)(2,1)S(1)}, u32[]{:S(2)}, u32[]{:S(2)}) %collective-permute-start.7) | collective-permute-done | bytes 196640 | tf_op jit(solution)/shard_map/ppermute | solution.py:350
  91.6 2.1 %collective-permute-done.8.value_ref = bf16[768,128]{1,0:T(8,128)(2,1)S(1)} collective-permute-done((bf16[768,128]{1,0:T(8,128)(2,1)S(1)}, bf16[768,128]{1,0:T(8,128)(2,1)S(1)}, u32[]{:S(2)}, u32[]{:S(2)}) %collective-permute-start.8) | collective-permute-done | bytes 196640 | tf_op jit(solution)/shard_map/ppermute | solution.py:351
  93.7 0.7 finish.1
  94.4 4.4 %collective-permute-start.9 = (bf16[96,512]{1,0:T(8,128)(2,1)S(1)}, bf16[96,512]{1,0:T(8,128)(2,1)S(1)}, u32[]{:S(2)}, u32[]{:S(2)}) collective-permute-start(bf16[96,512]{1,0:T(8,128)(2,1)S(1)} %get-tuple-element.18), channel_id=1, source_target_pairs={{0,8},{8,0},{16,24},{24,16},{32,40},{40,32},{48,56},{56,48},{64,72... | collective-permute-start | bytes 294920 | tf_op jit(solution)/shard_map/ppermute | solution.py:385
  98.8 0.9 collective-permute-done.9
  99.7 0.7 pad_maximum_fusion
  (3 shorter events, 0.1 us)
Async XLA Ops:
  3.0 41.5 %all-to-all-start = ((bf16[64,8,640]{2,1,0:T(8,128)(2,1)}), bf16[64,8,640]{2,1,0:T(8,128)(2,1)S(1)}, u32[]{:S(2)}, u32[]{:S(2)}) async-start(bf16[64,8,640]{2,1,0:T(8,128)(2,1)} %bitcast.16), calls=%async_computation | async-start | bytes 1310720 | tf_op jit(solution)/shard_map/all_to_all | solution.py:319
  61.0 6.4 %collective-permute-start.1 = (bf16[768,128]{1,0:T(8,128)(2,1)S(1)}, bf16[768,128]{1,0:T(8,128)(2,1)S(1)}, u32[]{:S(2)}, u32[]{:S(2)}) collective-permute-start(bf16[768,128]{1,0:T(8,128)(2,1)S(1)} %get-tuple-element.20.rest_0_), channel_id=1, source_target_pairs={{0,64},{64,128},{128,192},{192,256},{256,320},{320,384},{384,448},... | collective-permute-start | bytes 589832 | tf_op jit(solution)/shard_map/ppermute | solution.py:350
  62.3 7.2 %collective-permute-start.4 = (bf16[768,128]{1,0:T(8,128)(2,1)S(1)}, bf16[768,128]{1,0:T(8,128)(2,1)S(1)}, u32[]{:S(2)}, u32[]{:S(2)}) collective-permute-start(bf16[768,128]{1,0:T(8,128)(2,1)S(1)} %get-tuple-element.19.rest_4_), channel_id=1, source_target_pairs={{0,64},{64,128},{128,192},{192,256},{256,320},{320,384},{384,448},... | collective-permute-start | bytes 589832 | tf_op jit(solution)/shard_map/ppermute | solution.py:351
  67.4 6.4 %collective-permute-start.2 = (bf16[768,128]{1,0:T(8,128)(2,1)S(1)}, bf16[768,128]{1,0:T(8,128)(2,1)S(1)}, u32[]{:S(2)}, u32[]{:S(2)}) collective-permute-start(bf16[768,128]{1,0:T(8,128)(2,1)S(1)} %collective-permute-done.1.rest_1_), channel_id=1, source_target_pairs={{0,64},{64,128},{128,192},{192,256},{256,320},{320,384},{384,448},... | collective-permute-start | bytes 589832 | tf_op jit(solution)/shard_map/ppermute | solution.py:350
  69.5 6.5 %collective-permute-start.5 = (bf16[768,128]{1,0:T(8,128)(2,1)S(1)}, bf16[768,128]{1,0:T(8,128)(2,1)S(1)}, u32[]{:S(2)}, u32[]{:S(2)}) collective-permute-start(bf16[768,128]{1,0:T(8,128)(2,1)S(1)} %collective-permute-done.4.rest_5_), channel_id=1, source_target_pairs={{0,64},{64,128},{128,192},{192,256},{256,320},{320,384},{384,448},... | collective-permute-start | bytes 589832 | tf_op jit(solution)/shard_map/ppermute | solution.py:351
  73.8 11.3 %collective-permute-start.3 = (bf16[768,128]{1,0:T(8,128)(2,1)S(1)}, bf16[768,128]{1,0:T(8,128)(2,1)S(1)}, u32[]{:S(2)}, u32[]{:S(2)}) collective-permute-start(bf16[768,128]{1,0:T(8,128)(2,1)S(1)} %collective-permute-done.2.rest_2_), channel_id=1, source_target_pairs={{0,64},{64,128},{128,192},{192,256},{256,320},{320,384},{384,448},... | collective-permute-start | bytes 589832 | tf_op jit(solution)/shard_map/ppermute | solution.py:350
  76.0 10.4 %collective-permute-start.6 = (bf16[768,128]{1,0:T(8,128)(2,1)S(1)}, bf16[768,128]{1,0:T(8,128)(2,1)S(1)}, u32[]{:S(2)}, u32[]{:S(2)}) collective-permute-start(bf16[768,128]{1,0:T(8,128)(2,1)S(1)} %collective-permute-done.5.rest_6_), channel_id=1, source_target_pairs={{0,64},{64,128},{128,192},{192,256},{256,320},{320,384},{384,448},... | collective-permute-start | bytes 589832 | tf_op jit(solution)/shard_map/ppermute | solution.py:351
  77.9 9.9 %copy-start = (s32[16]{0:T(128)S(1)}, s32[16]{0:T(128)}, u32[]{:S(2)}) copy-start(s32[16]{0:T(128)} %lengths_ref.3) | copy-start | bytes 196
  77.9 9.8 %collective-permute-start = (bf16[96,512]{1,0:T(8,128)(2,1)S(1)}, bf16[96,512]{1,0:T(8,128)(2,1)S(1)}, u32[]{:S(2)}, u32[]{:S(2)}) collective-permute-start(bf16[96,512]{1,0:T(8,128)(2,1)S(1)} %get-tuple-element.13), channel_id=1, source_target_pairs={{0,8},{8,0},{16,24},{24,16},{32,40},{40,32},{48,56},{56,48},{64,72... | collective-permute-start | bytes 294920 | tf_op jit(solution)/shard_map/ppermute | solution.py:354
  85.1 6.4 %collective-permute-start.7 = (bf16[768,128]{1,0:T(8,128)(2,1)S(1)}, bf16[768,128]{1,0:T(8,128)(2,1)S(1)}, u32[]{:S(2)}, u32[]{:S(2)}) collective-permute-start(bf16[768,128]{1,0:T(8,128)(2,1)S(1)} %collective-permute-done.3.rest_3_), channel_id=1, source_target_pairs={{0,64},{64,128},{128,192},{192,256},{256,320},{320,384},{384,448},... | collective-permute-start | bytes 589832 | tf_op jit(solution)/shard_map/ppermute | solution.py:350
  86.5 7.2 %collective-permute-start.8 = (bf16[768,128]{1,0:T(8,128)(2,1)S(1)}, bf16[768,128]{1,0:T(8,128)(2,1)S(1)}, u32[]{:S(2)}, u32[]{:S(2)}) collective-permute-start(bf16[768,128]{1,0:T(8,128)(2,1)S(1)} %collective-permute-done.6.rest_7_), channel_id=1, source_target_pairs={{0,64},{64,128},{128,192},{192,256},{256,320},{320,384},{384,448},... | collective-permute-start | bytes 589832 | tf_op jit(solution)/shard_map/ppermute | solution.py:351
  94.4 5.3 %collective-permute-start.9 = (bf16[96,512]{1,0:T(8,128)(2,1)S(1)}, bf16[96,512]{1,0:T(8,128)(2,1)S(1)}, u32[]{:S(2)}, u32[]{:S(2)}) collective-permute-start(bf16[96,512]{1,0:T(8,128)(2,1)S(1)} %get-tuple-element.18), channel_id=1, source_target_pairs={{0,8},{8,0},{16,24},{24,16},{32,40},{40,32},{48,56},{56,48},{64,72... | collective-permute-start | bytes 294920 | tf_op jit(solution)/shard_map/ppermute | solution.py:385

commit v3 on v2

--- a/solution.py
+++ b/solution.py
@@ -98,7 +98,7 @@
         out_ref[:, part] = value.astype(jnp.bfloat16)
 
 
-def unpack_kernel(n, keys, index_ref, got_ref, *outs):
+def unpack_kernel(n, index_ref, got_ref, kv_ref, keep_ref, give_ref):
     rows = n * SLOTS
     tall = (n, rows)
     mark_row = iota(tall, 0) * SLOTS + CAP
@@ -122,44 +122,52 @@
         return hot(want == jnp.broadcast_to(place, wide))
 
     main = place_of(jnp.where(row < CAP, row, -1))
-    if keys:
-        (kv_ref,) = outs
-        tok = kv_ref.shape[0]
-        kv_ref[:, :HEAD_WIDTH] = times(pick(main, tok, 0), group(4)).astype(jnp.bfloat16)
-        v = sum(
-            times(pick(place_of(jnp.where(row >= CAP, row - CAP + first, -1)), tok, 0), group(at))
-            for at, first in ((4, 0), (0, 2), (1, 4))
-        )
-        kv_ref[:, HEAD_WIDTH:] = v.astype(jnp.bfloat16)
-        return
-    half, width = outs[0].shape
+    tok = kv_ref.shape[0]
+    kv_ref[:, :HEAD_WIDTH] = times(pick(main, tok, 0), group(4)).astype(jnp.bfloat16)
+    v = sum(
+        times(pick(place_of(jnp.where(row >= CAP, row - CAP + first, -1)), tok, 0), group(at))
+        for at, first in ((4, 0), (0, 2), (1, 4))
+    )
+    kv_ref[:, HEAD_WIDTH:] = v.astype(jnp.bfloat16)
+    half, width = keep_ref.shape
     even = index_ref[0] % 2 == 0
-    for ref, own in zip(outs, (even, jnp.logical_not(even))):
+    for ref, own in ((keep_ref, even), (give_ref, jnp.logical_not(even))):
         chosen = pick(main, half, jnp.where(own, 0, half))
         ref[...] = times(chosen, got_ref[:, :width]).astype(jnp.bfloat16)
 
 
-def attend_kernel(n, groups, lengths_ref, index_ref, q1_ref, q2_ref, *rest):
-    key_refs, value_refs = rest[:STEPS], rest[STEPS : 2 * STEPS]
-    heads_ref, top_ref, acc_ref, scores_ref = rest[2 * STEPS :]
-    half = q1_ref.shape[0]
-    tok = 2 * half
-    span = key_refs[0].shape[0]
+def attend_kernel(n, groups, steps, lengths_ref, index_ref, *refs):
+    count = len(steps)
+    begin = steps[0] == 0
+    given = 2 if begin else 3
+    key_refs = dict(zip(steps, refs[given : given + count]))
+    value_refs = dict(zip(steps, refs[given + count : given + 2 * count]))
+    if begin:
+        q1_ref, q2_ref = refs[:given]
+        heads_ref, top_ref, acc_ref, scores_ref = refs[given + 2 * count :]
+    else:
+        heads_ref, old_top_ref, old_acc_ref = refs[:given]
+        top_ref, acc_ref, scores_ref = refs[given + 2 * count :]
+    tok = heads_ref.shape[0] // groups
+    half = tok // 2
+    span = key_refs[steps[0]].shape[0]
     index = index_ref[0]
-    even = index % 2 == 0
-    chunk = jnp.where(even, index // 2, n - 1 - index // 2)
+    chunk = jnp.where(index % 2 == 0, index // 2, n - 1 - index // 2)
     first_row = chunk * tok
     run = first_row // span
-    scale = HEAD_WIDTH ** (-0.5) * math.log2(math.e)
-
-    for g in range(groups):
-        lanes = slice(g * HEAD_WIDTH, (g + 1) * HEAD_WIDTH)
-        for ref, at in ((q1_ref, g * tok), (q2_ref, g * tok + half)):
-            scaled = ref[:, lanes].astype(jnp.float32) * scale
-            upper = scaled.astype(jnp.bfloat16)
-            lower = (scaled - upper.astype(jnp.float32)).astype(jnp.bfloat16)
-            heads_ref[at : at + half, :HEAD_WIDTH] = upper
-            heads_ref[at : at + half, HEAD_WIDTH:] = lower
+
+    if begin:
+        scale = HEAD_WIDTH ** (-0.5) * math.log2(math.e)
+        for g in range(groups):
+            lanes = slice(g * HEAD_WIDTH, (g + 1) * HEAD_WIDTH)
+            for ref, at in ((q1_ref, g * tok), (q2_ref, g * tok + half)):
+                scaled = ref[:, lanes].astype(jnp.float32) * scale
+                upper = scaled.astype(jnp.bfloat16)
+                lower = (scaled - upper.astype(jnp.float32)).astype(jnp.bfloat16)
+                heads_ref[at : at + half, :HEAD_WIDTH] = upper
+                heads_ref[at : at + half, HEAD_WIDTH:] = lower
+    else:
+        top_ref[...] = old_top_ref[...]
 
     column = (tok, HEAD_WIDTH)
     query_pos = first_row + iota(column, 0)
@@ -174,66 +182,84 @@
     def score(step, base, masked):
         k = key_refs[step][...]
         k = jnp.concatenate([k, k], axis=1)
-        own = step == 0
         reach = span // HEAD_WIDTH
         if masked:
             key_pos = base + iota((tok, span), 1)
             allowed = key_pos >= jnp.concatenate([start] * reach, axis=1)
-            if own:
+            if step == 0:
                 allowed &= key_pos <= jnp.concatenate([query_pos] * reach, axis=1)
-        for g in range(groups):
-            rows = slice(g * tok, (g + 1) * tok)
-            s = times_t(heads_ref[rows, :], k)
+        for t0 in range(0, span, 256):
+            s = times_t(heads_ref[...], k[t0 : t0 + 256, :])
             if masked:
-                s = jnp.where(allowed, s, NEG)
-            scores_ref[rows, step * span : (step + 1) * span] = s
-            top = s[:, :HEAD_WIDTH]
-            for i in range(1, reach):
-                top = jnp.maximum(top, s[:, i * HEAD_WIDTH : (i + 1) * HEAD_WIDTH])
-            if not own:
-                top = jnp.maximum(top, top_ref[rows, :])
-            top_ref[rows, :] = top
+                part = allowed[:, t0 : t0 + 256]
+                s = jnp.where(jnp.concatenate([part] * groups, axis=0), s, NEG)
+            at = (step - steps[0]) * span + t0
+            scores_ref[:, at : at + 256] = s
+            top = jnp.maximum(s[:, :HEAD_WIDTH], s[:, HEAD_WIDTH:])
+            if step or t0:
+                top = jnp.maximum(top, top_ref[...])
+            top_ref[...] = top
 
     def weigh(step):
         v = value_refs[step][...]
         v = jnp.concatenate([v, jnp.ones_like(v)], axis=1)
-        for g in range(groups):
-            rows = slice(g * tok, (g + 1) * tok)
+        at = (step - steps[0]) * span
+        for r0 in range(0, groups * tok, 2 * tok):
+            rows = slice(r0, r0 + 2 * tok)
             top = jnp.concatenate([top_ref[rows, :]] * (span // HEAD_WIDTH), axis=1)
-            w = jnp.exp2(scores_ref[rows, step * span : (step + 1) * span] - top)
+            w = jnp.exp2(scores_ref[rows, at : at + span] - top)
             acc = times(w.astype(jnp.bfloat16), v)
             if step:
                 acc += acc_ref[rows, :]
             acc_ref[rows, :] = acc
 
-    bases = [(run - step) * span for step in range(STEPS)]
+    def base_of(step):
+        return (run - step) * span
 
     def needed(step):
-        return (bases[step] >= 0) & (bases[step] + span > first_start)
-
-    score(0, bases[0], True)
-    for step in range(1, STEPS):
-        clear = bases[step] >= last_start
+        return (base_of(step) >= 0) & (base_of(step) + span > first_start)
+
+    for step in steps:
+        if step == 0:
+            score(0, base_of(0), True)
+            continue
+        clear = base_of(step) >= last_start
 
         @pl.when(needed(step) & clear)
         def _(step=step):
-            score(step, bases[step], False)
+            score(step, base_of(step), False)
 
         @pl.when(needed(step) & jnp.logical_not(clear))
         def _(step=step):
-            score(step, bases[step], True)
-
-    for g in range(groups):
-        rows = slice(g * tok, (g + 1) * tok)
-        top = jnp.max(top_ref[rows, :], axis=1, keepdims=True)
-        top_ref[rows, :] = jnp.broadcast_to(top, column)
-
-    weigh(0)
-    for step in range(1, STEPS):
-
-        @pl.when(needed(step))
-        def _(step=step):
-            weigh(step)
+            score(step, base_of(step), True)
+
+    def settle():
+        for g in range(groups):
+            rows = slice(g * tok, (g + 1) * tok)
+            top = jnp.max(top_ref[rows, :], axis=1, keepdims=True)
+            top = jnp.broadcast_to(top, column)
+            top_ref[rows, :] = top
+            if not begin:
+                keep = jnp.exp2(old_top_ref[rows, :] - top)
+                acc_ref[rows, :] = old_acc_ref[rows, :] * jnp.concatenate([keep, keep], axis=1)
+
+    if begin:
+        settle()
+    else:
+        pl.when(needed(steps[0]))(settle)
+
+        @pl.when(jnp.logical_not(needed(steps[0])))
+        def _():
+            acc_ref[...] = old_acc_ref[...]
+
+    for step in steps:
+        if step == 0:
+            weigh(0)
+        else:
+
+            @pl.when(needed(step))
+            def _(step=step):
+                weigh(step)
 
 
 def finish_kernel(
@@ -320,20 +346,14 @@
 
     params = pltpu.CompilerParams(vmem_limit_bytes=48 * 2**20)
     part = jax.ShapeDtypeStruct((half, width), bf16)
-    got = got.reshape(rows, lanes)
-
-    def unpack(keys, *shapes):
-        return pl.pallas_call(
-            functools.partial(unpack_kernel, n, keys),
-            out_shape=shapes,
-            in_specs=[SMEM, VMEM],
-            out_specs=(VMEM,) * len(shapes),
-            compiler_params=params,
-            name="unpack_kv" if keys else "unpack_q",
-        )(here, got)
-
-    (my_kv,) = unpack(True, jax.ShapeDtypeStruct((tok, 2 * HEAD_WIDTH), bf16))
-    keep, give = unpack(False, part, part)
+    my_kv, keep, give = pl.pallas_call(
+        functools.partial(unpack_kernel, n),
+        out_shape=(jax.ShapeDtypeStruct((tok, 2 * HEAD_WIDTH), bf16), part, part),
+        in_specs=[SMEM, VMEM],
+        out_specs=(VMEM, VMEM, VMEM),
+        compiler_params=params,
+        name="unpack",
+    )(here, got.reshape(rows, lanes))
 
     planes = n // PLANE
     groups_of = [list(range(z * PLANE, (z + 1) * PLANE)) for z in range(planes)]
@@ -352,27 +372,35 @@
 
     swap = [(i, i ^ 1) for i in range(n)]
     taken = lax.ppermute(give, "ctx", swap)
+    scaled = jax.ShapeDtypeStruct((groups * tok, 2 * HEAD_WIDTH), bf16)
     sums = (
-        jax.ShapeDtypeStruct((groups * tok, 2 * HEAD_WIDTH), bf16),
         jax.ShapeDtypeStruct((groups * tok, HEAD_WIDTH), jnp.float32),
         jax.ShapeDtypeStruct((groups * tok, 2 * HEAD_WIDTH), jnp.float32),
     )
     params = pltpu.CompilerParams(vmem_limit_bytes=32 * 2**20)
     pairs = groups * tok * PLANE * half
-    state = pl.pallas_call(
-        functools.partial(attend_kernel, n, groups),
-        out_shape=sums,
-        in_specs=[SMEM, SMEM] + [VMEM] * (2 * STEPS + 2),
-        out_specs=(VMEM,) * 3,
-        scratch_shapes=[pltpu.VMEM((groups * tok, STEPS * PLANE * half), jnp.float32)],
-        compiler_params=params,
-        cost_estimate=pl.CostEstimate(
-            flops=64 * STEPS * HEAD_WIDTH * pairs,
-            bytes_accessed=2**23,
-            transcendentals=8 * STEPS * pairs,
-        ),
-        name="attend",
-    )(lengths, here, keep, taken, *run_keys[:STEPS], *run_values[:STEPS])
+
+    def attend(steps, *arrays):
+        arrays += tuple(run_keys[step] for step in steps)
+        arrays += tuple(run_values[step] for step in steps)
+        out = (scaled, *sums) if steps[0] == 0 else sums
+        return pl.pallas_call(
+            functools.partial(attend_kernel, n, groups, steps),
+            out_shape=out,
+            in_specs=[SMEM, SMEM] + [VMEM] * len(arrays),
+            out_specs=(VMEM,) * len(out),
+            scratch_shapes=[pltpu.VMEM((groups * tok, len(steps) * PLANE * half), jnp.float32)],
+            compiler_params=params,
+            cost_estimate=pl.CostEstimate(
+                flops=64 * len(steps) * HEAD_WIDTH * pairs,
+                bytes_accessed=2**23,
+                transcendentals=8 * len(steps) * pairs,
+            ),
+            name=f"attend{steps[0]}",
+        )(lengths, here, *arrays)
+
+    heads, *state = attend((0,), keep, taken)
+    state = (heads, *attend(tuple(range(1, STEPS)), heads, *state))
     first, second = pl.pallas_call(
         functools.partial(finish_kernel, n, groups),
         out_shape=(part, part),
@@ -382,9 +410,13 @@
         name="finish",
     )(lengths, here, *state, run_keys[STEPS], run_values[STEPS])
 
-    second = lax.ppermute(second, "ctx", swap)
-    return jnp.concatenate(
-        [jnp.where(even, first, second), jnp.where(even, second, first)], axis=0
+    others = lax.all_gather(
+        second, "ctx", axis_index_groups=[[i, i + 1] for i in range(0, n, 2)], axis=0
+    )
+    return jnp.where(
+        even,
+        jnp.concatenate([first, others[1]], axis=0),
+        jnp.concatenate([others[0], first], axis=0),
     )
 
 

time: 101 us -> 98.9 us (0.979)
  starting transfers between devices: 39.5 us -> 34.1 us
  blocking collectives: 15.3 us -> 20.1 us
  waiting for transfers between devices: 37.3 us -> 35.9 us
    all_gather x0 -> x1, blocking collectives: none -> 4.76 us  [local(): lax.all_gather(second, 'ctx', axis_index_groups=[[i, i + 1] for i in rang...]
    ppermute x1 -> x0, starting transfers between devices: 4.37 us -> none  [local(): second = lax.ppermute(second, 'ctx', swap)]
    ppermute x1, starting transfers between devices: 7.21 us -> 6.18 us  [local(): taken = lax.ppermute(give, 'ctx', swap)]
  transfers between devices with their start and end apart: 11 -> 10, of which waited for: 8 -> 7; matrix products, arithmetic and copies ran while one was open for 0% -> 0% of each run, Pallas kernels for 2% -> 2%
where the time goes in v3:
time: 98.9 us; the launch traced here: 98.5 us
  waiting for transfers between devices  35.9 us (36%)
  starting transfers between devices  34.1 us (34%)
  blocking collectives  20.1 us (20%)
  Pallas kernels  7.26 us (7%)
    all_to_all x1, waiting for transfers between devices, local(): lax.all_to_all(packed.reshape(n, SLOTS, lanes), 'ctx', 0, 0, tiled=True)  23.8 us
    all_to_all x1, starting transfers between devices, local(): lax.all_to_all(packed.reshape(n, SLOTS, lanes), 'ctx', 0, 0, tiled=True)  17.6 us
    all_gather x1, blocking collectives, local(): lax.all_gather(my_kv, 'ctx', axis_index_groups=groups_of, axis=0, tiled=T...  15.4 us
    ppermute x4, waiting for transfers between devices, local(): run_keys.append(lax.ppermute(run_keys[step], 'ctx', chain))  8.22 us
    ppermute x1, starting transfers between devices, local(): taken = lax.ppermute(give, 'ctx', swap)  6.18 us
    ppermute x4, starting transfers between devices, local(): run_values.append(lax.ppermute(run_values[step], 'ctx', chain))  5.15 us
    ppermute x4, starting transfers between devices, local(): run_keys.append(lax.ppermute(run_keys[step], 'ctx', chain))  5.15 us
    all_gather x1, blocking collectives, local(): lax.all_gather(second, 'ctx', axis_index_groups=[[i, i + 1] for i in rang...  4.76 us
  transfers between devices with their start and end apart: 10, of which 7 were waited for; matrix products, arithmetic and copies ran while one was open for 0% of the time, Pallas kernels for 2%

profile of v3, /device:TPU:1, one launch (start us, length us, event | category | flops | bytes accessed | tf_op | source)
XLA Modules:
  0.0 98.5 jit_solution(361943408606834440)
XLA Ops:
  0.0 3.0 %pack.1 = bf16[512,640]{1,0:T(8,128)(2,1)} custom-call(s32[1,192]{1,0:T(1,128)} %bitcast.17, bf16[192,512]{1,0:T(8,128)(2,1)} %q_hbm.1, bf16[192,128]{1,0:T(8,128)(2,1)} %k_hbm.1, bf16[192,128]{1,0:T(8,128)(2,1)} %v_hbm.1), custom_call_target="tpu_custom_call" | custom-call | tf_op jit(solution)/shard_map/pack/pallas_call | solution.py:330
  3.0 17.6 %all-to-all-start = ((bf16[64,8,640]{2,1,0:T(8,128)(2,1)}), bf16[64,8,640]{2,1,0:T(8,128)(2,1)S(1)}, u32[]{:S(2)}, u32[]{:S(2)}) async-start(bf16[64,8,640]{2,1,0:T(8,128)(2,1)} %bitcast.15), calls=%async_computation | async-start | bytes 1310720 | tf_op jit(solution)/shard_map/all_to_all | solution.py:345
  20.7 23.8 %all-to-all-done = bf16[64,8,640]{2,1,0:T(8,128)(2,1)S(1)} async-done(((bf16[64,8,640]{2,1,0:T(8,128)(2,1)}), bf16[64,8,640]{2,1,0:T(8,128)(2,1)S(1)}, u32[]{:S(2)}, u32[]{:S(2)}) %all-to-all-start) | async-done | bytes 655392 | tf_op jit(solution)/shard_map/all_to_all | solution.py:345
  44.5 1.1 %unpack.1 = (bf16[192,256]{1,0:T(8,128)(2,1)S(1)}, bf16[96,512]{1,0:T(8,128)(2,1)S(1)}, bf16[96,512]{1,0:T(8,128)(2,1)S(1)}) custom-call(s32[1]{0:T(128)} %bitcast.index_ref, bf16[512,640]{1,0:T(8,128)(2,1)S(1)} %bitcast.12), custom_call_target="tpu_custom_call" | custom-call | tf_op jit(solution)/shard_map/unpack/pallas_call | solution.py:349
  45.6 15.4 %all_gather.9 = bf16[1536,256]{1,0:T(8,128)(2,1)S(1)} all-gather(bf16[192,256]{1,0:T(8,128)(2,1)S(1)} %get-tuple-element.17), channel_id=1, replica_groups={{0,8,16,24,32,40,48,56},{64,72,80,88,96,104,112,120},{128,136,144,152,1..., dimensions={0}, use_global_device_ids=true | all-gather | bytes 884736 | tf_op jit(solution)/shard_map/all_gather | solution.py:360
  61.0 0.1 fusion
  61.2 1.3 %collective-permute-start.1 = (bf16[768,128]{1,0:T(8,128)(2,1)S(1)}, bf16[768,128]{1,0:T(8,128)(2,1)S(1)}, u32[]{:S(2)}, u32[]{:S(2)}) collective-permute-start(bf16[768,128]{1,0:T(8,128)(2,1)S(1)} %get-tuple-element.26.refs_2_), channel_id=1, source_target_pairs={{0,64},{64,128},{128,192},{192,256},{256,320},{320,384},{384,448},... | collective-permute-start | bytes 589832 | tf_op jit(solution)/shard_map/ppermute | solution.py:370
  62.5 1.3 %collective-permute-start.4 = (bf16[768,128]{1,0:T(8,128)(2,1)S(1)}, bf16[768,128]{1,0:T(8,128)(2,1)S(1)}, u32[]{:S(2)}, u32[]{:S(2)}) collective-permute-start(bf16[768,128]{1,0:T(8,128)(2,1)S(1)} %get-tuple-element.25.refs_3_), channel_id=1, source_target_pairs={{0,64},{64,128},{128,192},{192,256},{256,320},{320,384},{384,448},... | collective-permute-start | bytes 589832 | tf_op jit(solution)/shard_map/ppermute | solution.py:371
  63.8 3.8 %collective-permute-done.1.refs_3_ = bf16[768,128]{1,0:T(8,128)(2,1)S(1)} collective-permute-done((bf16[768,128]{1,0:T(8,128)(2,1)S(1)}, bf16[768,128]{1,0:T(8,128)(2,1)S(1)}, u32[]{:S(2)}, u32[]{:S(2)}) %collective-permute-start.1) | collective-permute-done | bytes 196640 | tf_op jit(solution)/shard_map/ppermute | solution.py:370
  67.6 1.3 %collective-permute-start.2 = (bf16[768,128]{1,0:T(8,128)(2,1)S(1)}, bf16[768,128]{1,0:T(8,128)(2,1)S(1)}, u32[]{:S(2)}, u32[]{:S(2)}) collective-permute-start(bf16[768,128]{1,0:T(8,128)(2,1)S(1)} %collective-permute-done.1.refs_3_), channel_id=1, source_target_pairs={{0,64},{64,128},{128,192},{192,256},{256,320},{320,384},{384,448},... | collective-permute-start | bytes 589832 | tf_op jit(solution)/shard_map/ppermute | solution.py:370
  68.9 0.8 collective-permute-done.4.refs_6_
  69.7 1.3 %collective-permute-start.5 = (bf16[768,128]{1,0:T(8,128)(2,1)S(1)}, bf16[768,128]{1,0:T(8,128)(2,1)S(1)}, u32[]{:S(2)}, u32[]{:S(2)}) collective-permute-start(bf16[768,128]{1,0:T(8,128)(2,1)S(1)} %collective-permute-done.4.refs_6_), channel_id=1, source_target_pairs={{0,64},{64,128},{128,192},{192,256},{256,320},{320,384},{384,448},... | collective-permute-start | bytes 589832 | tf_op jit(solution)/shard_map/ppermute | solution.py:371
  71.0 0.0 copy-start
  71.0 6.2 %collective-permute-start = (bf16[96,512]{1,0:T(8,128)(2,1)S(1)}, bf16[96,512]{1,0:T(8,128)(2,1)S(1)}, u32[]{:S(2)}, u32[]{:S(2)}) collective-permute-start(bf16[96,512]{1,0:T(8,128)(2,1)S(1)} %get-tuple-element.16), channel_id=1, source_target_pairs={{0,8},{8,0},{16,24},{24,16},{32,40},{40,32},{48,56},{56,48},{64,72... | collective-permute-start | bytes 294920 | tf_op jit(solution)/shard_map/ppermute | solution.py:374
  77.2 0.0 collective-permute-done.2.refs_4_
  77.2 1.3 %collective-permute-start.3 = (bf16[768,128]{1,0:T(8,128)(2,1)S(1)}, bf16[768,128]{1,0:T(8,128)(2,1)S(1)}, u32[]{:S(2)}, u32[]{:S(2)}) collective-permute-start(bf16[768,128]{1,0:T(8,128)(2,1)S(1)} %collective-permute-done.2.refs_4_), channel_id=1, source_target_pairs={{0,64},{64,128},{128,192},{192,256},{256,320},{320,384},{384,448},... | collective-permute-start | bytes 589832 | tf_op jit(solution)/shard_map/ppermute | solution.py:370
  78.5 0.0 collective-permute-done.5.refs_7_
  78.5 1.3 %collective-permute-start.6 = (bf16[768,128]{1,0:T(8,128)(2,1)S(1)}, bf16[768,128]{1,0:T(8,128)(2,1)S(1)}, u32[]{:S(2)}, u32[]{:S(2)}) collective-permute-start(bf16[768,128]{1,0:T(8,128)(2,1)S(1)} %collective-permute-done.5.refs_7_), channel_id=1, source_target_pairs={{0,64},{64,128},{128,192},{192,256},{256,320},{320,384},{384,448},... | collective-permute-start | bytes 589832 | tf_op jit(solution)/shard_map/ppermute | solution.py:371
  79.8 0.0 collective-permute-done.refs_1_
  79.8 0.0 copy-done
  79.8 1.6 %attend0.1 = (bf16[768,256]{1,0:T(8,128)(2,1)S(1)}, f32[768,128]{1,0:T(8,128)S(1)}, f32[768,256]{1,0:T(8,128)S(1)}) custom-call(s32[16]{0:T(128)S(1)} %copy-done, s32[1]{0:T(128)} %bitcast.index_ref, bf16[96,512]{1,0:T(8,128)(2,1)S(1)} %get-tuple-element.15.refs_0_, bf16[96,512]{1,0:T(8,128)(2,1)S(1)} %collective-permute-done.refs_1_, ...), custom_call_target="tpu_custom_call" | custom-call | flops 4831838208 | bytes 8388608 | tf_op jit(solution)/shard_map/attend0/pallas_call | solution.py:387
  81.4 2.2 %collective-permute-done.3.refs_5_ = bf16[768,128]{1,0:T(8,128)(2,1)S(1)} collective-permute-done((bf16[768,128]{1,0:T(8,128)(2,1)S(1)}, bf16[768,128]{1,0:T(8,128)(2,1)S(1)}, u32[]{:S(2)}, u32[]{:S(2)}) %collective-permute-start.3) | collective-permute-done | bytes 196640 | tf_op jit(solution)/shard_map/ppermute | solution.py:370
  83.6 1.3 %collective-permute-start.7 = (bf16[768,128]{1,0:T(8,128)(2,1)S(1)}, bf16[768,128]{1,0:T(8,128)(2,1)S(1)}, u32[]{:S(2)}, u32[]{:S(2)}) collective-permute-start(bf16[768,128]{1,0:T(8,128)(2,1)S(1)} %collective-permute-done.3.refs_5_), channel_id=1, source_target_pairs={{0,64},{64,128},{128,192},{192,256},{256,320},{320,384},{384,448},... | collective-permute-start | bytes 589832 | tf_op jit(solution)/shard_map/ppermute | solution.py:370
  84.9 0.8 collective-permute-done.6.refs_8_
  85.7 1.3 %collective-permute-start.8 = (bf16[768,128]{1,0:T(8,128)(2,1)S(1)}, bf16[768,128]{1,0:T(8,128)(2,1)S(1)}, u32[]{:S(2)}, u32[]{:S(2)}) collective-permute-start(bf16[768,128]{1,0:T(8,128)(2,1)S(1)} %collective-permute-done.6.refs_8_), channel_id=1, source_target_pairs={{0,64},{64,128},{128,192},{192,256},{256,320},{320,384},{384,448},... | collective-permute-start | bytes 589832 | tf_op jit(solution)/shard_map/ppermute | solution.py:371
  87.0 0.8 attend1.1
  87.8 2.2 %collective-permute-done.7.key_ref = bf16[768,128]{1,0:T(8,128)(2,1)S(1)} collective-permute-done((bf16[768,128]{1,0:T(8,128)(2,1)S(1)}, bf16[768,128]{1,0:T(8,128)(2,1)S(1)}, u32[]{:S(2)}, u32[]{:S(2)}) %collective-permute-start.7) | collective-permute-done | bytes 196640 | tf_op jit(solution)/shard_map/ppermute | solution.py:370
  90.0 2.2 %collective-permute-done.8.value_ref = bf16[768,128]{1,0:T(8,128)(2,1)S(1)} collective-permute-done((bf16[768,128]{1,0:T(8,128)(2,1)S(1)}, bf16[768,128]{1,0:T(8,128)(2,1)S(1)}, u32[]{:S(2)}, u32[]{:S(2)}) %collective-permute-start.8) | collective-permute-done | bytes 196640 | tf_op jit(solution)/shard_map/ppermute | solution.py:371
  92.2 0.7 finish.1
  93.0 4.8 %all-gather = bf16[192,512]{1,0:T(8,128)(2,1)S(1)} all-gather(bf16[96,512]{1,0:T(8,128)(2,1)S(1)} %get-tuple-element.24), channel_id=2, replica_groups={{0,8},{16,24},{32,40},{48,56},{64,72},{80,88},{96,104},{112,120},{128,1..., dimensions={0}, use_global_device_ids=true | all-gather | bytes 294912 | tf_op jit(solution)/shard_map/all_gather | solution.py:413
  97.7 0.7 maximum_select_fusion
  (3 shorter events, 0.1 us)
Async XLA Ops:
  3.0 41.5 %all-to-all-start = ((bf16[64,8,640]{2,1,0:T(8,128)(2,1)}), bf16[64,8,640]{2,1,0:T(8,128)(2,1)S(1)}, u32[]{:S(2)}, u32[]{:S(2)}) async-start(bf16[64,8,640]{2,1,0:T(8,128)(2,1)} %bitcast.15), calls=%async_computation | async-start | bytes 1310720 | tf_op jit(solution)/shard_map/all_to_all | solution.py:345
  61.2 6.4 %collective-permute-start.1 = (bf16[768,128]{1,0:T(8,128)(2,1)S(1)}, bf16[768,128]{1,0:T(8,128)(2,1)S(1)}, u32[]{:S(2)}, u32[]{:S(2)}) collective-permute-start(bf16[768,128]{1,0:T(8,128)(2,1)S(1)} %get-tuple-element.26.refs_2_), channel_id=1, source_target_pairs={{0,64},{64,128},{128,192},{192,256},{256,320},{320,384},{384,448},... | collective-permute-start | bytes 589832 | tf_op jit(solution)/shard_map/ppermute | solution.py:370
  62.5 7.2 %collective-permute-start.4 = (bf16[768,128]{1,0:T(8,128)(2,1)S(1)}, bf16[768,128]{1,0:T(8,128)(2,1)S(1)}, u32[]{:S(2)}, u32[]{:S(2)}) collective-permute-start(bf16[768,128]{1,0:T(8,128)(2,1)S(1)} %get-tuple-element.25.refs_3_), channel_id=1, source_target_pairs={{0,64},{64,128},{128,192},{192,256},{256,320},{320,384},{384,448},... | collective-permute-start | bytes 589832 | tf_op jit(solution)/shard_map/ppermute | solution.py:371
  67.6 9.6 %collective-permute-start.2 = (bf16[768,128]{1,0:T(8,128)(2,1)S(1)}, bf16[768,128]{1,0:T(8,128)(2,1)S(1)}, u32[]{:S(2)}, u32[]{:S(2)}) collective-permute-start(bf16[768,128]{1,0:T(8,128)(2,1)S(1)} %collective-permute-done.1.refs_3_), channel_id=1, source_target_pairs={{0,64},{64,128},{128,192},{192,256},{256,320},{320,384},{384,448},... | collective-permute-start | bytes 589832 | tf_op jit(solution)/shard_map/ppermute | solution.py:370
  69.7 8.8 %collective-permute-start.5 = (bf16[768,128]{1,0:T(8,128)(2,1)S(1)}, bf16[768,128]{1,0:T(8,128)(2,1)S(1)}, u32[]{:S(2)}, u32[]{:S(2)}) collective-permute-start(bf16[768,128]{1,0:T(8,128)(2,1)S(1)} %collective-permute-done.4.refs_6_), channel_id=1, source_target_pairs={{0,64},{64,128},{128,192},{192,256},{256,320},{320,384},{384,448},... | collective-permute-start | bytes 589832 | tf_op jit(solution)/shard_map/ppermute | solution.py:371
  71.0 8.8 %copy-start = (s32[16]{0:T(128)S(1)}, s32[16]{0:T(128)}, u32[]{:S(2)}) copy-start(s32[16]{0:T(128)} %lengths_ref.5) | copy-start | bytes 196
  71.0 8.8 %collective-permute-start = (bf16[96,512]{1,0:T(8,128)(2,1)S(1)}, bf16[96,512]{1,0:T(8,128)(2,1)S(1)}, u32[]{:S(2)}, u32[]{:S(2)}) collective-permute-start(bf16[96,512]{1,0:T(8,128)(2,1)S(1)} %get-tuple-element.16), channel_id=1, source_target_pairs={{0,8},{8,0},{16,24},{24,16},{32,40},{40,32},{48,56},{56,48},{64,72... | collective-permute-start | bytes 294920 | tf_op jit(solution)/shard_map/ppermute | solution.py:374
  77.2 6.4 %collective-permute-start.3 = (bf16[768,128]{1,0:T(8,128)(2,1)S(1)}, bf16[768,128]{1,0:T(8,128)(2,1)S(1)}, u32[]{:S(2)}, u32[]{:S(2)}) collective-permute-start(bf16[768,128]{1,0:T(8,128)(2,1)S(1)} %collective-permute-done.2.refs_4_), channel_id=1, source_target_pairs={{0,64},{64,128},{128,192},{192,256},{256,320},{320,384},{384,448},... | collective-permute-start | bytes 589832 | tf_op jit(solution)/shard_map/ppermute | solution.py:370
  78.5 7.2 %collective-permute-start.6 = (bf16[768,128]{1,0:T(8,128)(2,1)S(1)}, bf16[768,128]{1,0:T(8,128)(2,1)S(1)}, u32[]{:S(2)}, u32[]{:S(2)}) collective-permute-start(bf16[768,128]{1,0:T(8,128)(2,1)S(1)} %collective-permute-done.5.refs_7_), channel_id=1, source_target_pairs={{0,64},{64,128},{128,192},{192,256},{256,320},{320,384},{384,448},... | collective-permute-start | bytes 589832 | tf_op jit(solution)/shard_map/ppermute | solution.py:371
  83.6 6.4 %collective-permute-start.7 = (bf16[768,128]{1,0:T(8,128)(2,1)S(1)}, bf16[768,128]{1,0:T(8,128)(2,1)S(1)}, u32[]{:S(2)}, u32[]{:S(2)}) collective-permute-start(bf16[768,128]{1,0:T(8,128)(2,1)S(1)} %collective-permute-done.3.refs_5_), channel_id=1, source_target_pairs={{0,64},{64,128},{128,192},{192,256},{256,320},{320,384},{384,448},... | collective-permute-start | bytes 589832 | tf_op jit(solution)/shard_map/ppermute | solution.py:370
  85.7 6.5 %collective-permute-start.8 = (bf16[768,128]{1,0:T(8,128)(2,1)S(1)}, bf16[768,128]{1,0:T(8,128)(2,1)S(1)}, u32[]{:S(2)}, u32[]{:S(2)}) collective-permute-start(bf16[768,128]{1,0:T(8,128)(2,1)S(1)} %collective-permute-done.6.refs_8_), channel_id=1, source_target_pairs={{0,64},{64,128},{128,192},{192,256},{256,320},{320,384},{384,448},... | collective-permute-start | bytes 589832 | tf_op jit(solution)/shard_map/ppermute | solution.py:371

commit v4 on v3

--- a/solution.py
+++ b/solution.py
@@ -56,37 +56,35 @@
     slot = route - owner * tok
     square = (tok, tok)
     down, across = iota(square, 0), iota(square, 1)
-    along = jnp.broadcast_to(owner, square)
-    column = jnp.sum(jnp.where(down == across, along, 0), axis=1, keepdims=True)
-    order = jnp.sum(
-        jnp.where((column == along) & (down < across), 1, 0), axis=0, keepdims=True
-    )
+    route_col = jnp.sum(
+        jnp.where(down == across, jnp.broadcast_to(route, square), 0), axis=1, keepdims=True
+    )
+    owner_col = divide(route_col, tok)
+    same = owner_col == jnp.broadcast_to(owner, square)
+    order = jnp.sum(jnp.where(same & (down < across), 1, 0), axis=0, keepdims=True)
+    order_col = jnp.sum(jnp.where(same & (across < down), 1, 0), axis=1, keepdims=True)
     wide = (rows, tok)
     line = iota(wide, 0)
-    to = owner * SLOTS
-
-    def pick(row, valid=None):
-        where_to = to + row
-        if valid is not None:
-            where_to = jnp.where(valid, where_to, -1)
-        return hot(line == jnp.broadcast_to(where_to, wide))
-
-    value_picks = {
-        group: pick(CAP + order - first, (order >= first) & (order < first + 2))
-        for group, first in ((4, 0), (0, 2), (1, 4))
-    }
-    lanes = (HEAD_WIDTH, tok)
-    places = jnp.where(
-        iota(lanes, 0) == jnp.broadcast_to(order, lanes),
-        jnp.broadcast_to(slot + 1, lanes).astype(jnp.float32),
-        jnp.float32(0),
-    ).astype(jnp.bfloat16)
-    extra = {2: times_t(pick(CAP), places)}
+
+    def pick(row):
+        return hot(line == jnp.broadcast_to(owner * SLOTS + row, wide))
+
+    spare = pick(CAP + (order & 1))
+    column = (tok, HEAD_WIDTH)
+    order_wide = jnp.broadcast_to(order_col, column)
+    place = jnp.where(
+        iota(column, 1) == order_wide, (route_col - owner_col * tok + 1).astype(jnp.float32), 0.0
+    )
     main = pick(order)
     copies[1].wait()
     copies[2].wait()
-    for group, chosen in value_picks.items():
-        extra[group] = times(chosen, v_ref[...])
+    v = v_ref[...].astype(jnp.float32)
+    pieces = [jnp.where((order_wide >> 1) == i, v, 0.0) for i in range(3)] + [place]
+    extra = times(spare, jnp.concatenate(pieces, axis=1).astype(jnp.bfloat16))
+    extra = {
+        group: extra[:, i * HEAD_WIDTH : (i + 1) * HEAD_WIDTH]
+        for i, group in enumerate((4, 0, 1, 2))
+    }
     extra[4] += times(main, k_ref[...])
     copies[3].wait()
     packed = times(main, q_ref[...])
@@ -106,7 +104,8 @@
     def group(i):
         return got_ref[:, i * HEAD_WIDTH : (i + 1) * HEAD_WIDTH]
 
-    marks = times(hot(iota(tall, 1) == mark_row), group(2)).astype(jnp.bfloat16)
+    marked = (iota(tall, 1) == mark_row) | (iota(tall, 1) == mark_row + 1)
+    marks = times(hot(marked), group(2)).astype(jnp.bfloat16)
     mine = iota(tall, 1) - iota(tall, 0) * SLOTS
     mine = (mine >= 0) & (mine < SLOTS)
     lanes = (HEAD_WIDTH, rows)
@@ -263,7 +262,7 @@
 
 
 def finish_kernel(
-    n, groups, lengths_ref, index_ref, heads_ref, top_ref, acc_ref, key_ref, value_ref, first_ref, second_ref
+    n, groups, lengths_ref, index_ref, heads_ref, top_ref, acc_ref, key_ref, value_ref, first_ref, second_ref, scores_ref, new_top_ref
 ):
     tok = heads_ref.shape[0] // groups
     half = tok // 2
@@ -294,20 +293,23 @@
         k, v = key_ref[...], value_ref[...]
         k = jnp.concatenate([k, k], axis=1)
         v = jnp.concatenate([v, jnp.ones_like(v)], axis=1)
-        key_pos = base + iota((tok, span), 1)
-        allowed = key_pos >= jnp.concatenate([start] * reach, axis=1)
-        for g in range(groups):
-            rows = slice(g * tok, (g + 1) * tok)
-            s = jnp.where(allowed, times_t(heads_ref[rows, :], k), NEG)
-            top = s[:, :HEAD_WIDTH]
-            for i in range(1, reach):
-                top = jnp.maximum(top, s[:, i * HEAD_WIDTH : (i + 1) * HEAD_WIDTH])
-            top = jnp.broadcast_to(jnp.max(top, axis=1, keepdims=True), column)
-            before = top_ref[rows, :]
-            top = jnp.maximum(top, before)
-            w = jnp.exp2(s - jnp.concatenate([top] * reach, axis=1)).astype(jnp.bfloat16)
-            keep = jnp.exp2(before - top)
-            write(g, times(w, v) + acc_ref[rows, :] * jnp.concatenate([keep, keep], axis=1))
+        for t0 in range(0, span, 256):
+            s = times_t(heads_ref[...], k[t0 : t0 + 256, :])
+            allowed = base + t0 + iota((tok, 256), 1) >= jnp.concatenate([start] * 2, axis=1)
+            s = jnp.where(jnp.concatenate([allowed] * groups, axis=0), s, NEG)
+            scores_ref[:, t0 : t0 + 256] = s
+            top = jnp.maximum(s[:, :HEAD_WIDTH], s[:, HEAD_WIDTH:])
+            new_top_ref[...] = jnp.maximum(top, new_top_ref[...] if t0 else top_ref[...])
+        for g in range(0, groups, 2):
+            rows = slice(g * tok, (g + 2) * tok)
+            top = jnp.max(new_top_ref[rows, :], axis=1, keepdims=True)
+            top = jnp.broadcast_to(top, (2 * tok, HEAD_WIDTH))
+            w = jnp.exp2(scores_ref[rows, :] - jnp.concatenate([top] * reach, axis=1))
+            keep = jnp.exp2(top_ref[rows, :] - top)
+            acc = times(w.astype(jnp.bfloat16), v)
+            acc += acc_ref[rows, :] * jnp.concatenate([keep, keep], axis=1)
+            write(g, acc[:tok])
+            write(g + 1, acc[tok:])
 
     @pl.when(jnp.logical_not(needed))
     def _():
@@ -406,6 +408,10 @@
         out_shape=(part, part),
         in_specs=[SMEM, SMEM] + [VMEM] * 5,
         out_specs=(VMEM, VMEM),
+        scratch_shapes=[
+            pltpu.VMEM((groups * tok, PLANE * half), jnp.float32),
+            pltpu.VMEM((groups * tok, HEAD_WIDTH), jnp.float32),
+        ],
         compiler_params=params,
         name="finish",
     )(lengths, here, *state, run_keys[STEPS], run_values[STEPS])

time: 98.9 us -> 98.4 us (level)
  waiting for transfers between devices: 35.9 us -> 34.9 us
    pallas_call x2, Pallas kernels: 2.37 us -> 3.39 us  [attend(): pl.pallas_call(functools.partial(attend_kernel, n, groups, steps), out_sh...]
    ppermute x4, waiting for transfers between devices: 8.22 us -> 7.21 us  [local(): run_keys.append(lax.ppermute(run_keys[step], 'ctx', chain))]
  transfers between devices with their start and end apart: 10 -> 10, of which waited for: 7 -> 7; matrix products, arithmetic and copies ran while one was open for 0% -> 0% of each run, Pallas kernels for 2% -> 3%
where the time goes in v4:
time: 98.4 us; the launch traced here: 97.9 us
  waiting for transfers between devices  34.9 us (35%)
  starting transfers between devices  34.1 us (35%)
  blocking collectives  20.1 us (20%)
  Pallas kernels  7.81 us (8%)
    all_to_all x1, waiting for transfers between devices, local(): lax.all_to_all(packed.reshape(n, SLOTS, lanes), 'ctx', 0, 0, tiled=True)  23.8 us
    all_to_all x1, starting transfers between devices, local(): lax.all_to_all(packed.reshape(n, SLOTS, lanes), 'ctx', 0, 0, tiled=True)  17.6 us
    all_gather x1, blocking collectives, local(): lax.all_gather(my_kv, 'ctx', axis_index_groups=groups_of, axis=0, tiled=T...  15.3 us
    ppermute x4, waiting for transfers between devices, local(): run_keys.append(lax.ppermute(run_keys[step], 'ctx', chain))  7.21 us
    ppermute x1, starting transfers between devices, local(): taken = lax.ppermute(give, 'ctx', swap)  6.16 us
    ppermute x4, starting transfers between devices, local(): run_values.append(lax.ppermute(run_values[step], 'ctx', chain))  5.15 us
    ppermute x4, starting transfers between devices, local(): run_keys.append(lax.ppermute(run_keys[step], 'ctx', chain))  5.15 us
    all_gather x1, blocking collectives, local(): lax.all_gather(second, 'ctx', axis_index_groups=[[i, i + 1] for i in rang...  4.72 us
  transfers between devices with their start and end apart: 10, of which 7 were waited for; matrix products, arithmetic and copies ran while one was open for 0% of the time, Pallas kernels for 3%

profile of v4, /device:TPU:1, one launch (start us, length us, event | category | flops | bytes accessed | tf_op | source)
XLA Modules:
  0.0 97.9 jit_solution(3143511355364850654)
XLA Ops:
  0.0 2.6 %pack.1 = bf16[512,640]{1,0:T(8,128)(2,1)} custom-call(s32[1,192]{1,0:T(1,128)} %bitcast.17, bf16[192,512]{1,0:T(8,128)(2,1)} %q_hbm.1, bf16[192,128]{1,0:T(8,128)(2,1)} %k_hbm.1, bf16[192,128]{1,0:T(8,128)(2,1)} %v_hbm.1), custom_call_target="tpu_custom_call" | custom-call | tf_op jit(solution)/shard_map/pack/pallas_call | solution.py:332
  2.6 17.6 %all-to-all-start = ((bf16[64,8,640]{2,1,0:T(8,128)(2,1)}), bf16[64,8,640]{2,1,0:T(8,128)(2,1)S(1)}, u32[]{:S(2)}, u32[]{:S(2)}) async-start(bf16[64,8,640]{2,1,0:T(8,128)(2,1)} %bitcast.15), calls=%async_computation | async-start | bytes 1310720 | tf_op jit(solution)/shard_map/all_to_all | solution.py:347
  20.2 23.8 %all-to-all-done = bf16[64,8,640]{2,1,0:T(8,128)(2,1)S(1)} async-done(((bf16[64,8,640]{2,1,0:T(8,128)(2,1)}), bf16[64,8,640]{2,1,0:T(8,128)(2,1)S(1)}, u32[]{:S(2)}, u32[]{:S(2)}) %all-to-all-start) | async-done | bytes 655392 | tf_op jit(solution)/shard_map/all_to_all | solution.py:347
  44.0 1.1 %unpack.1 = (bf16[192,256]{1,0:T(8,128)(2,1)S(1)}, bf16[96,512]{1,0:T(8,128)(2,1)S(1)}, bf16[96,512]{1,0:T(8,128)(2,1)S(1)}) custom-call(s32[1]{0:T(128)} %bitcast.index_ref, bf16[512,640]{1,0:T(8,128)(2,1)S(1)} %bitcast.12), custom_call_target="tpu_custom_call" | custom-call | tf_op jit(solution)/shard_map/unpack/pallas_call | solution.py:351
  45.2 15.3 %all_gather.9 = bf16[1536,256]{1,0:T(8,128)(2,1)S(1)} all-gather(bf16[192,256]{1,0:T(8,128)(2,1)S(1)} %get-tuple-element.17), channel_id=1, replica_groups={{0,8,16,24,32,40,48,56},{64,72,80,88,96,104,112,120},{128,136,144,152,1..., dimensions={0}, use_global_device_ids=true | all-gather | bytes 884736 | tf_op jit(solution)/shard_map/all_gather | solution.py:362
  60.5 0.1 fusion
  60.7 1.3 %collective-permute-start.1 = (bf16[768,128]{1,0:T(8,128)(2,1)S(1)}, bf16[768,128]{1,0:T(8,128)(2,1)S(1)}, u32[]{:S(2)}, u32[]{:S(2)}) collective-permute-start(bf16[768,128]{1,0:T(8,128)(2,1)S(1)} %get-tuple-element.26.refs_2_), channel_id=1, source_target_pairs={{0,64},{64,128},{128,192},{192,256},{256,320},{320,384},{384,448},... | collective-permute-start | bytes 589832 | tf_op jit(solution)/shard_map/ppermute | solution.py:372
  62.0 1.3 %collective-permute-start.4 = (bf16[768,128]{1,0:T(8,128)(2,1)S(1)}, bf16[768,128]{1,0:T(8,128)(2,1)S(1)}, u32[]{:S(2)}, u32[]{:S(2)}) collective-permute-start(bf16[768,128]{1,0:T(8,128)(2,1)S(1)} %get-tuple-element.25.refs_3_), channel_id=1, source_target_pairs={{0,64},{64,128},{128,192},{192,256},{256,320},{320,384},{384,448},... | collective-permute-start | bytes 589832 | tf_op jit(solution)/shard_map/ppermute | solution.py:373
  63.3 3.8 %collective-permute-done.1.refs_3_ = bf16[768,128]{1,0:T(8,128)(2,1)S(1)} collective-permute-done((bf16[768,128]{1,0:T(8,128)(2,1)S(1)}, bf16[768,128]{1,0:T(8,128)(2,1)S(1)}, u32[]{:S(2)}, u32[]{:S(2)}) %collective-permute-start.1) | collective-permute-done | bytes 196640 | tf_op jit(solution)/shard_map/ppermute | solution.py:372
  67.1 1.3 %collective-permute-start.2 = (bf16[768,128]{1,0:T(8,128)(2,1)S(1)}, bf16[768,128]{1,0:T(8,128)(2,1)S(1)}, u32[]{:S(2)}, u32[]{:S(2)}) collective-permute-start(bf16[768,128]{1,0:T(8,128)(2,1)S(1)} %collective-permute-done.1.refs_3_), channel_id=1, source_target_pairs={{0,64},{64,128},{128,192},{192,256},{256,320},{320,384},{384,448},... | collective-permute-start | bytes 589832 | tf_op jit(solution)/shard_map/ppermute | solution.py:372
  68.4 0.8 collective-permute-done.4.refs_6_
  69.2 1.3 %collective-permute-start.5 = (bf16[768,128]{1,0:T(8,128)(2,1)S(1)}, bf16[768,128]{1,0:T(8,128)(2,1)S(1)}, u32[]{:S(2)}, u32[]{:S(2)}) collective-permute-start(bf16[768,128]{1,0:T(8,128)(2,1)S(1)} %collective-permute-done.4.refs_6_), channel_id=1, source_target_pairs={{0,64},{64,128},{128,192},{192,256},{256,320},{320,384},{384,448},... | collective-permute-start | bytes 589832 | tf_op jit(solution)/shard_map/ppermute | solution.py:373
  70.5 0.0 copy-start
  70.5 6.2 %collective-permute-start = (bf16[96,512]{1,0:T(8,128)(2,1)S(1)}, bf16[96,512]{1,0:T(8,128)(2,1)S(1)}, u32[]{:S(2)}, u32[]{:S(2)}) collective-permute-start(bf16[96,512]{1,0:T(8,128)(2,1)S(1)} %get-tuple-element.16), channel_id=1, source_target_pairs={{0,8},{8,0},{16,24},{24,16},{32,40},{40,32},{48,56},{56,48},{64,72... | collective-permute-start | bytes 294920 | tf_op jit(solution)/shard_map/ppermute | solution.py:376
  76.7 0.0 collective-permute-done.2.refs_4_
  76.7 1.3 %collective-permute-start.3 = (bf16[768,128]{1,0:T(8,128)(2,1)S(1)}, bf16[768,128]{1,0:T(8,128)(2,1)S(1)}, u32[]{:S(2)}, u32[]{:S(2)}) collective-permute-start(bf16[768,128]{1,0:T(8,128)(2,1)S(1)} %collective-permute-done.2.refs_4_), channel_id=1, source_target_pairs={{0,64},{64,128},{128,192},{192,256},{256,320},{320,384},{384,448},... | collective-permute-start | bytes 589832 | tf_op jit(solution)/shard_map/ppermute | solution.py:372
  78.0 0.0 collective-permute-done.5.refs_7_
  78.0 1.3 %collective-permute-start.6 = (bf16[768,128]{1,0:T(8,128)(2,1)S(1)}, bf16[768,128]{1,0:T(8,128)(2,1)S(1)}, u32[]{:S(2)}, u32[]{:S(2)}) collective-permute-start(bf16[768,128]{1,0:T(8,128)(2,1)S(1)} %collective-permute-done.5.refs_7_), channel_id=1, source_target_pairs={{0,64},{64,128},{128,192},{192,256},{256,320},{320,384},{384,448},... | collective-permute-start | bytes 589832 | tf_op jit(solution)/shard_map/ppermute | solution.py:373
  79.3 0.0 collective-permute-done.refs_1_
  79.3 0.0 copy-done
  79.3 1.6 %attend0.1 = (bf16[768,256]{1,0:T(8,128)(2,1)S(1)}, f32[768,128]{1,0:T(8,128)S(1)}, f32[768,256]{1,0:T(8,128)S(1)}) custom-call(s32[16]{0:T(128)S(1)} %copy-done, s32[1]{0:T(128)} %bitcast.index_ref, bf16[96,512]{1,0:T(8,128)(2,1)S(1)} %get-tuple-element.15.refs_0_, bf16[96,512]{1,0:T(8,128)(2,1)S(1)} %collective-permute-done.refs_1_, ...), custom_call_target="tpu_custom_call" | custom-call | flops 4831838208 | bytes 8388608 | tf_op jit(solution)/shard_map/attend0/pallas_call | solution.py:389
  80.9 2.2 %collective-permute-done.3.refs_5_ = bf16[768,128]{1,0:T(8,128)(2,1)S(1)} collective-permute-done((bf16[768,128]{1,0:T(8,128)(2,1)S(1)}, bf16[768,128]{1,0:T(8,128)(2,1)S(1)}, u32[]{:S(2)}, u32[]{:S(2)}) %collective-permute-start.3) | collective-permute-done | bytes 196640 | tf_op jit(solution)/shard_map/ppermute | solution.py:372
  83.1 1.3 %collective-permute-start.7 = (bf16[768,128]{1,0:T(8,128)(2,1)S(1)}, bf16[768,128]{1,0:T(8,128)(2,1)S(1)}, u32[]{:S(2)}, u32[]{:S(2)}) collective-permute-start(bf16[768,128]{1,0:T(8,128)(2,1)S(1)} %collective-permute-done.3.refs_5_), channel_id=1, source_target_pairs={{0,64},{64,128},{128,192},{192,256},{256,320},{320,384},{384,448},... | collective-permute-start | bytes 589832 | tf_op jit(solution)/shard_map/ppermute | solution.py:372
  84.4 0.8 collective-permute-done.6.refs_8_
  85.2 1.3 %collective-permute-start.8 = (bf16[768,128]{1,0:T(8,128)(2,1)S(1)}, bf16[768,128]{1,0:T(8,128)(2,1)S(1)}, u32[]{:S(2)}, u32[]{:S(2)}) collective-permute-start(bf16[768,128]{1,0:T(8,128)(2,1)S(1)} %collective-permute-done.6.refs_8_), channel_id=1, source_target_pairs={{0,64},{64,128},{128,192},{192,256},{256,320},{320,384},{384,448},... | collective-permute-start | bytes 589832 | tf_op jit(solution)/shard_map/ppermute | solution.py:373
  86.5 1.8 %attend1.1 = (f32[768,128]{1,0:T(8,128)S(1)}, f32[768,256]{1,0:T(8,128)S(1)}) custom-call(s32[16]{0:T(128)S(1)} %copy-done, s32[1]{0:T(128)} %bitcast.index_ref, bf16[768,256]{1,0:T(8,128)(2,1)S(1)} %get-tuple-element.18.refs_0_.heads_ref, f32[768,128]{1,0:T(8,128)S(1)} %get-tuple-element.19.refs_1_, f32[768,256]{1,0:T(8,128)S(1)} %get-tuple-element.20.refs_2_, ...), custom_call_target="tpu_custom_call" | custom-call | flops 14495514624 | bytes 8388608 | tf_op jit(solution)/shard_map/attend1/pallas_call | solution.py:389
  88.3 1.2 %collective-permute-done.7.key_ref = bf16[768,128]{1,0:T(8,128)(2,1)S(1)} collective-permute-done((bf16[768,128]{1,0:T(8,128)(2,1)S(1)}, bf16[768,128]{1,0:T(8,128)(2,1)S(1)}, u32[]{:S(2)}, u32[]{:S(2)}) %collective-permute-start.7) | collective-permute-done | bytes 196640 | tf_op jit(solution)/shard_map/ppermute | solution.py:372
  89.5 2.2 %collective-permute-done.8.value_ref = bf16[768,128]{1,0:T(8,128)(2,1)S(1)} collective-permute-done((bf16[768,128]{1,0:T(8,128)(2,1)S(1)}, bf16[768,128]{1,0:T(8,128)(2,1)S(1)}, u32[]{:S(2)}, u32[]{:S(2)}) %collective-permute-start.8) | collective-permute-done | bytes 196640 | tf_op jit(solution)/shard_map/ppermute | solution.py:373
  91.7 0.7 finish.1
  92.5 4.7 %all-gather = bf16[192,512]{1,0:T(8,128)(2,1)S(1)} all-gather(bf16[96,512]{1,0:T(8,128)(2,1)S(1)} %get-tuple-element.24), channel_id=2, replica_groups={{0,8},{16,24},{32,40},{48,56},{64,72},{80,88},{96,104},{112,120},{128,1..., dimensions={0}, use_global_device_ids=true | all-gather | bytes 294912 | tf_op jit(solution)/shard_map/all_gather | solution.py:419
  97.2 0.7 maximum_select_fusion
  (3 shorter events, 0.1 us)
Async XLA Ops:
  2.6 41.4 %all-to-all-start = ((bf16[64,8,640]{2,1,0:T(8,128)(2,1)}), bf16[64,8,640]{2,1,0:T(8,128)(2,1)S(1)}, u32[]{:S(2)}, u32[]{:S(2)}) async-start(bf16[64,8,640]{2,1,0:T(8,128)(2,1)} %bitcast.15), calls=%async_computation | async-start | bytes 1310720 | tf_op jit(solution)/shard_map/all_to_all | solution.py:347
  60.7 6.4 %collective-permute-start.1 = (bf16[768,128]{1,0:T(8,128)(2,1)S(1)}, bf16[768,128]{1,0:T(8,128)(2,1)S(1)}, u32[]{:S(2)}, u32[]{:S(2)}) collective-permute-start(bf16[768,128]{1,0:T(8,128)(2,1)S(1)} %get-tuple-element.26.refs_2_), channel_id=1, source_target_pairs={{0,64},{64,128},{128,192},{192,256},{256,320},{320,384},{384,448},... | collective-permute-start | bytes 589832 | tf_op jit(solution)/shard_map/ppermute | solution.py:372
  62.0 7.2 %collective-permute-start.4 = (bf16[768,128]{1,0:T(8,128)(2,1)S(1)}, bf16[768,128]{1,0:T(8,128)(2,1)S(1)}, u32[]{:S(2)}, u32[]{:S(2)}) collective-permute-start(bf16[768,128]{1,0:T(8,128)(2,1)S(1)} %get-tuple-element.25.refs_3_), channel_id=1, source_target_pairs={{0,64},{64,128},{128,192},{192,256},{256,320},{320,384},{384,448},... | collective-permute-start | bytes 589832 | tf_op jit(solution)/shard_map/ppermute | solution.py:373
  67.1 9.6 %collective-permute-start.2 = (bf16[768,128]{1,0:T(8,128)(2,1)S(1)}, bf16[768,128]{1,0:T(8,128)(2,1)S(1)}, u32[]{:S(2)}, u32[]{:S(2)}) collective-permute-start(bf16[768,128]{1,0:T(8,128)(2,1)S(1)} %collective-permute-done.1.refs_3_), channel_id=1, source_target_pairs={{0,64},{64,128},{128,192},{192,256},{256,320},{320,384},{384,448},... | collective-permute-start | bytes 589832 | tf_op jit(solution)/shard_map/ppermute | solution.py:372
  69.2 8.8 %collective-permute-start.5 = (bf16[768,128]{1,0:T(8,128)(2,1)S(1)}, bf16[768,128]{1,0:T(8,128)(2,1)S(1)}, u32[]{:S(2)}, u32[]{:S(2)}) collective-permute-start(bf16[768,128]{1,0:T(8,128)(2,1)S(1)} %collective-permute-done.4.refs_6_), channel_id=1, source_target_pairs={{0,64},{64,128},{128,192},{192,256},{256,320},{320,384},{384,448},... | collective-permute-start | bytes 589832 | tf_op jit(solution)/shard_map/ppermute | solution.py:373
  70.5 8.8 %copy-start = (s32[16]{0:T(128)S(1)}, s32[16]{0:T(128)}, u32[]{:S(2)}) copy-start(s32[16]{0:T(128)} %lengths_ref.5) | copy-start | bytes 196
  70.5 8.8 %collective-permute-start = (bf16[96,512]{1,0:T(8,128)(2,1)S(1)}, bf16[96,512]{1,0:T(8,128)(2,1)S(1)}, u32[]{:S(2)}, u32[]{:S(2)}) collective-permute-start(bf16[96,512]{1,0:T(8,128)(2,1)S(1)} %get-tuple-element.16), channel_id=1, source_target_pairs={{0,8},{8,0},{16,24},{24,16},{32,40},{40,32},{48,56},{56,48},{64,72... | collective-permute-start | bytes 294920 | tf_op jit(solution)/shard_map/ppermute | solution.py:376
  76.7 6.4 %collective-permute-start.3 = (bf16[768,128]{1,0:T(8,128)(2,1)S(1)}, bf16[768,128]{1,0:T(8,128)(2,1)S(1)}, u32[]{:S(2)}, u32[]{:S(2)}) collective-permute-start(bf16[768,128]{1,0:T(8,128)(2,1)S(1)} %collective-permute-done.2.refs_4_), channel_id=1, source_target_pairs={{0,64},{64,128},{128,192},{192,256},{256,320},{320,384},{384,448},... | collective-permute-start | bytes 589832 | tf_op jit(solution)/shard_map/ppermute | solution.py:372
  78.0 7.2 %collective-permute-start.6 = (bf16[768,128]{1,0:T(8,128)(2,1)S(1)}, bf16[768,128]{1,0:T(8,128)(2,1)S(1)}, u32[]{:S(2)}, u32[]{:S(2)}) collective-permute-start(bf16[768,128]{1,0:T(8,128)(2,1)S(1)} %collective-permute-done.5.refs_7_), channel_id=1, source_target_pairs={{0,64},{64,128},{128,192},{192,256},{256,320},{320,384},{384,448},... | collective-permute-start | bytes 589832 | tf_op jit(solution)/shard_map/ppermute | solution.py:373
  83.1 6.4 %collective-permute-start.7 = (bf16[768,128]{1,0:T(8,128)(2,1)S(1)}, bf16[768,128]{1,0:T(8,128)(2,1)S(1)}, u32[]{:S(2)}, u32[]{:S(2)}) collective-permute-start(bf16[768,128]{1,0:T(8,128)(2,1)S(1)} %collective-permute-done.3.refs_5_), channel_id=1, source_target_pairs={{0,64},{64,128},{128,192},{192,256},{256,320},{320,384},{384,448},... | collective-permute-start | bytes 589832 | tf_op jit(solution)/shard_map/ppermute | solution.py:372
  85.2 6.5 %collective-permute-start.8 = (bf16[768,128]{1,0:T(8,128)(2,1)S(1)}, bf16[768,128]{1,0:T(8,128)(2,1)S(1)}, u32[]{:S(2)}, u32[]{:S(2)}) collective-permute-start(bf16[768,128]{1,0:T(8,128)(2,1)S(1)} %collective-permute-done.6.refs_8_), channel_id=1, source_target_pairs={{0,64},{64,128},{128,192},{192,256},{256,320},{320,384},{384,448},... | collective-permute-start | bytes 589832 | tf_op jit(solution)/shard_map/ppermute | solution.py:373

commit v5 on v4

--- a/solution.py
+++ b/solution.py
@@ -261,51 +261,72 @@
                 weigh(step)
 
 
-def finish_kernel(
-    n, groups, lengths_ref, index_ref, heads_ref, top_ref, acc_ref, key_ref, value_ref, first_ref, second_ref, scores_ref, new_top_ref
-):
-    tok = heads_ref.shape[0] // groups
-    half = tok // 2
-    span = key_ref.shape[0]
-    reach = span // HEAD_WIDTH
+def reach_of(n, tok, span, lengths_ref, index_ref):
     index = index_ref[0]
-    chunk = jnp.where(index % 2 == 0, index // 2, n - 1 - index // 2)
-    first_row = chunk * tok
-    base = (first_row // span - STEPS) * span
-    column = (tok, HEAD_WIDTH)
-    start = jnp.zeros(column, jnp.int32)
+    first_row = jnp.where(index % 2 == 0, index // 2, n - 1 - index // 2) * tok
     first_start = end = jnp.int32(0)
     for i in range(lengths_ref.shape[0]):
         end = end + lengths_ref[i]
-        start = jnp.where(first_row + iota(column, 0) >= end, end, start)
         first_start = jnp.where(first_row >= end, end, first_start)
-
-    def write(g, acc):
-        lanes = slice(g * HEAD_WIDTH, (g + 1) * HEAD_WIDTH)
-        out = (acc[:, :HEAD_WIDTH] / acc[:, HEAD_WIDTH:]).astype(jnp.bfloat16)
-        first_ref[:, lanes] = out[:half]
-        second_ref[:, lanes] = out[half:]
-
-    needed = (base >= 0) & (base + span > first_start)
+    base = (first_row // span - STEPS) * span
+    return first_row, base, (base >= 0) & (base + span > first_start)
+
+
+def far_score_kernel(n, groups, lengths_ref, index_ref, heads_ref, old_top_ref, key_ref, scores_ref, top_ref):
+    tok = heads_ref.shape[0] // groups
+    span = key_ref.shape[0]
+    first_row, base, needed = reach_of(n, tok, span, lengths_ref, index_ref)
 
     @pl.when(needed)
     def _():
-        k, v = key_ref[...], value_ref[...]
+        column = (tok, HEAD_WIDTH)
+        start = jnp.zeros(column, jnp.int32)
+        end = jnp.int32(0)
+        for i in range(lengths_ref.shape[0]):
+            end = end + lengths_ref[i]
+            start = jnp.where(first_row + iota(column, 0) >= end, end, start)
+        k = key_ref[...]
         k = jnp.concatenate([k, k], axis=1)
-        v = jnp.concatenate([v, jnp.ones_like(v)], axis=1)
         for t0 in range(0, span, 256):
             s = times_t(heads_ref[...], k[t0 : t0 + 256, :])
             allowed = base + t0 + iota((tok, 256), 1) >= jnp.concatenate([start] * 2, axis=1)
             s = jnp.where(jnp.concatenate([allowed] * groups, axis=0), s, NEG)
             scores_ref[:, t0 : t0 + 256] = s
             top = jnp.maximum(s[:, :HEAD_WIDTH], s[:, HEAD_WIDTH:])
-            new_top_ref[...] = jnp.maximum(top, new_top_ref[...] if t0 else top_ref[...])
+            top_ref[...] = jnp.maximum(top, top_ref[...] if t0 else old_top_ref[...])
+        for g in range(groups):
+            rows = slice(g * tok, (g + 1) * tok)
+            top = jnp.max(top_ref[rows, :], axis=1, keepdims=True)
+            top_ref[rows, :] = jnp.broadcast_to(top, column)
+
+    @pl.when(jnp.logical_not(needed))
+    def _():
+        top_ref[...] = old_top_ref[...]
+
+
+def finish_kernel(
+    n, groups, lengths_ref, index_ref, value_ref, scores_ref, old_top_ref, top_ref, acc_ref, first_ref, second_ref
+):
+    tok = acc_ref.shape[0] // groups
+    half = tok // 2
+    span = value_ref.shape[0]
+    _, _, needed = reach_of(n, tok, span, lengths_ref, index_ref)
+
+    def write(g, acc):
+        lanes = slice(g * HEAD_WIDTH, (g + 1) * HEAD_WIDTH)
+        out = (acc[:, :HEAD_WIDTH] / acc[:, HEAD_WIDTH:]).astype(jnp.bfloat16)
+        first_ref[:, lanes] = out[:half]
+        second_ref[:, lanes] = out[half:]
+
+    @pl.when(needed)
+    def _():
+        v = value_ref[...]
+        v = jnp.concatenate([v, jnp.ones_like(v)], axis=1)
         for g in range(0, groups, 2):
             rows = slice(g * tok, (g + 2) * tok)
-            top = jnp.max(new_top_ref[rows, :], axis=1, keepdims=True)
-            top = jnp.broadcast_to(top, (2 * tok, HEAD_WIDTH))
-            w = jnp.exp2(scores_ref[rows, :] - jnp.concatenate([top] * reach, axis=1))
-            keep = jnp.exp2(top_ref[rows, :] - top)
+            top = top_ref[rows, :]
+            w = jnp.exp2(scores_ref[rows, :] - jnp.concatenate([top] * (span // HEAD_WIDTH), axis=1))
+            keep = jnp.exp2(old_top_ref[rows, :] - top)
             acc = times(w.astype(jnp.bfloat16), v)
             acc += acc_ref[rows, :] * jnp.concatenate([keep, keep], axis=1)
             write(g, acc[:tok])
@@ -402,19 +423,23 @@
         )(lengths, here, *arrays)
 
     heads, *state = attend((0,), keep, taken)
-    state = (heads, *attend(tuple(range(1, STEPS)), heads, *state))
+    top, acc = attend(tuple(range(1, STEPS)), heads, *state)
+    scores, new_top = pl.pallas_call(
+        functools.partial(far_score_kernel, n, groups),
+        out_shape=(jax.ShapeDtypeStruct((groups * tok, PLANE * half), jnp.float32), sums[0]),
+        in_specs=[SMEM, SMEM] + [VMEM] * 3,
+        out_specs=(VMEM, VMEM),
+        compiler_params=params,
+        name="far_score",
+    )(lengths, here, heads, top, run_keys[STEPS])
     first, second = pl.pallas_call(
         functools.partial(finish_kernel, n, groups),
         out_shape=(part, part),
         in_specs=[SMEM, SMEM] + [VMEM] * 5,
         out_specs=(VMEM, VMEM),
-        scratch_shapes=[
-            pltpu.VMEM((groups * tok, PLANE * half), jnp.float32),
-            pltpu.VMEM((groups * tok, HEAD_WIDTH), jnp.float32),
-        ],
         compiler_params=params,
         name="finish",
-    )(lengths, here, *state, run_keys[STEPS], run_values[STEPS])
+    )(lengths, here, run_values[STEPS], scores, top, new_top, acc)
 
     others = lax.all_gather(
         second, "ctx", axis_index_groups=[[i, i + 1] for i in range(0, n, 2)], axis=0

time: 98.4 us -> 98.3 us (level)
    ppermute x4, waiting for transfers between devices: 7.21 us -> 8.26 us  [local(): run_keys.append(lax.ppermute(run_keys[step], 'ctx', chain))]
    pallas_call x2, Pallas kernels: 3.39 us -> 2.34 us  [attend(): pl.pallas_call(functools.partial(attend_kernel, n, groups, steps), out_sh...]
where the time goes in v5:
time: 98.3 us; the launch traced here: 97.8 us
  waiting for transfers between devices  35.3 us (36%)
  starting transfers between devices  34.1 us (35%)
  blocking collectives  20.1 us (20%)
  Pallas kernels  7.3 us (7%)
    all_to_all x1, waiting for transfers between devices, local(): lax.all_to_all(packed.reshape(n, SLOTS, lanes), 'ctx', 0, 0, tiled=True)  23.8 us
    all_to_all x1, starting transfers between devices, local(): lax.all_to_all(packed.reshape(n, SLOTS, lanes), 'ctx', 0, 0, tiled=True)  17.6 us
    all_gather x1, blocking collectives, local(): lax.all_gather(my_kv, 'ctx', axis_index_groups=groups_of, axis=0, tiled=T...  15.3 us
    ppermute x4, waiting for transfers between devices, local(): run_keys.append(lax.ppermute(run_keys[step], 'ctx', chain))  8.26 us
    ppermute x1, starting transfers between devices, local(): taken = lax.ppermute(give, 'ctx', swap)  6.12 us
    ppermute x4, starting transfers between devices, local(): run_keys.append(lax.ppermute(run_keys[step], 'ctx', chain))  5.15 us
    ppermute x4, starting transfers between devices, local(): run_values.append(lax.ppermute(run_values[step], 'ctx', chain))  5.15 us
    all_gather x1, blocking collectives, local(): lax.all_gather(second, 'ctx', axis_index_groups=[[i, i + 1] for i in rang...  4.74 us
  transfers between devices with their start and end apart: 10, of which 7 were waited for; matrix products, arithmetic and copies ran while one was open for 0% of the time, Pallas kernels for 3%

profile of v5, /device:TPU:1, one launch (start us, length us, event | category | flops | bytes accessed | tf_op | source)
XLA Modules:
  0.0 97.8 jit_solution(10719028278679702024)
XLA Ops:
  0.0 2.6 %pack.1 = bf16[512,640]{1,0:T(8,128)(2,1)} custom-call(s32[1,192]{1,0:T(1,128)} %bitcast.17, bf16[192,512]{1,0:T(8,128)(2,1)} %q_hbm.1, bf16[192,128]{1,0:T(8,128)(2,1)} %k_hbm.1, bf16[192,128]{1,0:T(8,128)(2,1)} %v_hbm.1), custom_call_target="tpu_custom_call" | custom-call | tf_op jit(solution)/shard_map/pack/pallas_call | solution.py:353
  2.6 17.6 %all-to-all-start = ((bf16[64,8,640]{2,1,0:T(8,128)(2,1)}), bf16[64,8,640]{2,1,0:T(8,128)(2,1)S(1)}, u32[]{:S(2)}, u32[]{:S(2)}) async-start(bf16[64,8,640]{2,1,0:T(8,128)(2,1)} %bitcast.15), calls=%async_computation | async-start | bytes 1310720 | tf_op jit(solution)/shard_map/all_to_all | solution.py:368
  20.2 0.0 copy-start
  20.3 23.8 %all-to-all-done = bf16[64,8,640]{2,1,0:T(8,128)(2,1)S(1)} async-done(((bf16[64,8,640]{2,1,0:T(8,128)(2,1)}), bf16[64,8,640]{2,1,0:T(8,128)(2,1)S(1)}, u32[]{:S(2)}, u32[]{:S(2)}) %all-to-all-start) | async-done | bytes 655392 | tf_op jit(solution)/shard_map/all_to_all | solution.py:368
  44.0 1.2 %unpack.1 = (bf16[192,256]{1,0:T(8,128)(2,1)S(1)}, bf16[96,512]{1,0:T(8,128)(2,1)S(1)}, bf16[96,512]{1,0:T(8,128)(2,1)S(1)}) custom-call(s32[1]{0:T(128)} %bitcast.index_ref, bf16[512,640]{1,0:T(8,128)(2,1)S(1)} %bitcast.12), custom_call_target="tpu_custom_call" | custom-call | tf_op jit(solution)/shard_map/unpack/pallas_call | solution.py:372
  45.2 15.3 %all_gather.9 = bf16[1536,256]{1,0:T(8,128)(2,1)S(1)} all-gather(bf16[192,256]{1,0:T(8,128)(2,1)S(1)} %get-tuple-element.17), channel_id=1, replica_groups={{0,8,16,24,32,40,48,56},{64,72,80,88,96,104,112,120},{128,136,144,152,1..., dimensions={0}, use_global_device_ids=true | all-gather | bytes 884736 | tf_op jit(solution)/shard_map/all_gather | solution.py:383
  60.5 0.1 fusion
  60.7 1.3 %collective-permute-start.5 = (bf16[768,128]{1,0:T(8,128)(2,1)S(1)}, bf16[768,128]{1,0:T(8,128)(2,1)S(1)}, u32[]{:S(2)}, u32[]{:S(2)}) collective-permute-start(bf16[768,128]{1,0:T(8,128)(2,1)S(1)} %get-tuple-element.29.refs_2_), channel_id=1, source_target_pairs={{0,64},{64,128},{128,192},{192,256},{256,320},{320,384},{384,448},... | collective-permute-start | bytes 589832 | tf_op jit(solution)/shard_map/ppermute | solution.py:393
  62.0 1.3 %collective-permute-start = (bf16[768,128]{1,0:T(8,128)(2,1)S(1)}, bf16[768,128]{1,0:T(8,128)(2,1)S(1)}, u32[]{:S(2)}, u32[]{:S(2)}) collective-permute-start(bf16[768,128]{1,0:T(8,128)(2,1)S(1)} %get-tuple-element.30.refs_3_), channel_id=1, source_target_pairs={{0,64},{64,128},{128,192},{192,256},{256,320},{320,384},{384,448},... | collective-permute-start | bytes 589832 | tf_op jit(solution)/shard_map/ppermute | solution.py:394
  63.3 3.8 %collective-permute-done.5.refs_3_ = bf16[768,128]{1,0:T(8,128)(2,1)S(1)} collective-permute-done((bf16[768,128]{1,0:T(8,128)(2,1)S(1)}, bf16[768,128]{1,0:T(8,128)(2,1)S(1)}, u32[]{:S(2)}, u32[]{:S(2)}) %collective-permute-start.5) | collective-permute-done | bytes 196640 | tf_op jit(solution)/shard_map/ppermute | solution.py:393
  67.1 1.3 %collective-permute-start.6 = (bf16[768,128]{1,0:T(8,128)(2,1)S(1)}, bf16[768,128]{1,0:T(8,128)(2,1)S(1)}, u32[]{:S(2)}, u32[]{:S(2)}) collective-permute-start(bf16[768,128]{1,0:T(8,128)(2,1)S(1)} %collective-permute-done.5.refs_3_), channel_id=1, source_target_pairs={{0,64},{64,128},{128,192},{192,256},{256,320},{320,384},{384,448},... | collective-permute-start | bytes 589832 | tf_op jit(solution)/shard_map/ppermute | solution.py:393
  68.4 0.8 collective-permute-done.refs_6_
  69.2 1.3 %collective-permute-start.1 = (bf16[768,128]{1,0:T(8,128)(2,1)S(1)}, bf16[768,128]{1,0:T(8,128)(2,1)S(1)}, u32[]{:S(2)}, u32[]{:S(2)}) collective-permute-start(bf16[768,128]{1,0:T(8,128)(2,1)S(1)} %collective-permute-done.refs_6_), channel_id=1, source_target_pairs={{0,64},{64,128},{128,192},{192,256},{256,320},{320,384},{384,448},... | collective-permute-start | bytes 589832 | tf_op jit(solution)/shard_map/ppermute | solution.py:394
  70.5 6.1 %collective-permute-start.4 = (bf16[96,512]{1,0:T(8,128)(2,1)S(1)}, bf16[96,512]{1,0:T(8,128)(2,1)S(1)}, u32[]{:S(2)}, u32[]{:S(2)}) collective-permute-start(bf16[96,512]{1,0:T(8,128)(2,1)S(1)} %get-tuple-element.19), channel_id=1, source_target_pairs={{0,8},{8,0},{16,24},{24,16},{32,40},{40,32},{48,56},{56,48},{64,72... | collective-permute-start | bytes 294920 | tf_op jit(solution)/shard_map/ppermute | solution.py:397
  76.6 0.0 collective-permute-done.6.refs_4_
  76.6 1.3 %collective-permute-start.7 = (bf16[768,128]{1,0:T(8,128)(2,1)S(1)}, bf16[768,128]{1,0:T(8,128)(2,1)S(1)}, u32[]{:S(2)}, u32[]{:S(2)}) collective-permute-start(bf16[768,128]{1,0:T(8,128)(2,1)S(1)} %collective-permute-done.6.refs_4_), channel_id=1, source_target_pairs={{0,64},{64,128},{128,192},{192,256},{256,320},{320,384},{384,448},... | collective-permute-start | bytes 589832 | tf_op jit(solution)/shard_map/ppermute | solution.py:393
  77.9 0.0 collective-permute-done.1.refs_7_
  77.9 1.3 %collective-permute-start.2 = (bf16[768,128]{1,0:T(8,128)(2,1)S(1)}, bf16[768,128]{1,0:T(8,128)(2,1)S(1)}, u32[]{:S(2)}, u32[]{:S(2)}) collective-permute-start(bf16[768,128]{1,0:T(8,128)(2,1)S(1)} %collective-permute-done.1.refs_7_), channel_id=1, source_target_pairs={{0,64},{64,128},{128,192},{192,256},{256,320},{320,384},{384,448},... | collective-permute-start | bytes 589832 | tf_op jit(solution)/shard_map/ppermute | solution.py:394
  79.2 0.0 collective-permute-done.4.refs_1_
  79.3 0.0 copy-done
  79.3 1.6 %attend0.1 = (bf16[768,256]{1,0:T(8,128)(2,1)S(1)}, f32[768,128]{1,0:T(8,128)S(1)}, f32[768,256]{1,0:T(8,128)S(1)}) custom-call(s32[16]{0:T(128)S(1)} %copy-done, s32[1]{0:T(128)} %bitcast.index_ref, bf16[96,512]{1,0:T(8,128)(2,1)S(1)} %get-tuple-element.18.refs_0_, bf16[96,512]{1,0:T(8,128)(2,1)S(1)} %collective-permute-done.4.refs_1_, ...), custom_call_target="tpu_custom_call" | custom-call | flops 4831838208 | bytes 8388608 | tf_op jit(solution)/shard_map/attend0/pallas_call | solution.py:410
  80.8 2.2 %collective-permute-done.7.refs_5_ = bf16[768,128]{1,0:T(8,128)(2,1)S(1)} collective-permute-done((bf16[768,128]{1,0:T(8,128)(2,1)S(1)}, bf16[768,128]{1,0:T(8,128)(2,1)S(1)}, u32[]{:S(2)}, u32[]{:S(2)}) %collective-permute-start.7) | collective-permute-done | bytes 196640 | tf_op jit(solution)/shard_map/ppermute | solution.py:393
  83.1 1.3 %collective-permute-start.8 = (bf16[768,128]{1,0:T(8,128)(2,1)S(1)}, bf16[768,128]{1,0:T(8,128)(2,1)S(1)}, u32[]{:S(2)}, u32[]{:S(2)}) collective-permute-start(bf16[768,128]{1,0:T(8,128)(2,1)S(1)} %collective-permute-done.7.refs_5_), channel_id=1, source_target_pairs={{0,64},{64,128},{128,192},{192,256},{256,320},{320,384},{384,448},... | collective-permute-start | bytes 589832 | tf_op jit(solution)/shard_map/ppermute | solution.py:393
  84.3 0.8 collective-permute-done.2.refs_8_
  85.2 1.3 %collective-permute-start.3 = (bf16[768,128]{1,0:T(8,128)(2,1)S(1)}, bf16[768,128]{1,0:T(8,128)(2,1)S(1)}, u32[]{:S(2)}, u32[]{:S(2)}) collective-permute-start(bf16[768,128]{1,0:T(8,128)(2,1)S(1)} %collective-permute-done.2.refs_8_), channel_id=1, source_target_pairs={{0,64},{64,128},{128,192},{192,256},{256,320},{320,384},{384,448},... | collective-permute-start | bytes 589832 | tf_op jit(solution)/shard_map/ppermute | solution.py:394
  86.4 0.8 attend1.1
  87.2 2.2 %collective-permute-done.8.key_ref = bf16[768,128]{1,0:T(8,128)(2,1)S(1)} collective-permute-done((bf16[768,128]{1,0:T(8,128)(2,1)S(1)}, bf16[768,128]{1,0:T(8,128)(2,1)S(1)}, u32[]{:S(2)}, u32[]{:S(2)}) %collective-permute-start.8) | collective-permute-done | bytes 196640 | tf_op jit(solution)/shard_map/ppermute | solution.py:393
  89.5 0.6 far_score.1
  90.1 1.6 %collective-permute-done.3.value_ref = bf16[768,128]{1,0:T(8,128)(2,1)S(1)} collective-permute-done((bf16[768,128]{1,0:T(8,128)(2,1)S(1)}, bf16[768,128]{1,0:T(8,128)(2,1)S(1)}, u32[]{:S(2)}, u32[]{:S(2)}) %collective-permute-start.3) | collective-permute-done | bytes 196640 | tf_op jit(solution)/shard_map/ppermute | solution.py:394
  91.7 0.6 finish.1
  92.3 4.7 %all-gather = bf16[192,512]{1,0:T(8,128)(2,1)S(1)} all-gather(bf16[96,512]{1,0:T(8,128)(2,1)S(1)} %get-tuple-element.28), channel_id=2, replica_groups={{0,8},{16,24},{32,40},{48,56},{64,72},{80,88},{96,104},{112,120},{128,1..., dimensions={0}, use_global_device_ids=true | all-gather | bytes 294912 | tf_op jit(solution)/shard_map/all_gather | solution.py:444
  97.1 0.7 maximum_select_fusion
  (3 shorter events, 0.1 us)
Async XLA Ops:
  2.6 41.4 %all-to-all-start = ((bf16[64,8,640]{2,1,0:T(8,128)(2,1)}), bf16[64,8,640]{2,1,0:T(8,128)(2,1)S(1)}, u32[]{:S(2)}, u32[]{:S(2)}) async-start(bf16[64,8,640]{2,1,0:T(8,128)(2,1)} %bitcast.15), calls=%async_computation | async-start | bytes 1310720 | tf_op jit(solution)/shard_map/all_to_all | solution.py:368
  20.2 59.0 %copy-start = (s32[16]{0:T(128)S(1)}, s32[16]{0:T(128)}, u32[]{:S(2)}) copy-start(s32[16]{0:T(128)} %lengths_ref.7) | copy-start | bytes 196
  60.7 6.4 %collective-permute-start.5 = (bf16[768,128]{1,0:T(8,128)(2,1)S(1)}, bf16[768,128]{1,0:T(8,128)(2,1)S(1)}, u32[]{:S(2)}, u32[]{:S(2)}) collective-permute-start(bf16[768,128]{1,0:T(8,128)(2,1)S(1)} %get-tuple-element.29.refs_2_), channel_id=1, source_target_pairs={{0,64},{64,128},{128,192},{192,256},{256,320},{320,384},{384,448},... | collective-permute-start | bytes 589832 | tf_op jit(solution)/shard_map/ppermute | solution.py:393
  62.0 7.2 %collective-permute-start = (bf16[768,128]{1,0:T(8,128)(2,1)S(1)}, bf16[768,128]{1,0:T(8,128)(2,1)S(1)}, u32[]{:S(2)}, u32[]{:S(2)}) collective-permute-start(bf16[768,128]{1,0:T(8,128)(2,1)S(1)} %get-tuple-element.30.refs_3_), channel_id=1, source_target_pairs={{0,64},{64,128},{128,192},{192,256},{256,320},{320,384},{384,448},... | collective-permute-start | bytes 589832 | tf_op jit(solution)/shard_map/ppermute | solution.py:394
  67.1 9.5 %collective-permute-start.6 = (bf16[768,128]{1,0:T(8,128)(2,1)S(1)}, bf16[768,128]{1,0:T(8,128)(2,1)S(1)}, u32[]{:S(2)}, u32[]{:S(2)}) collective-permute-start(bf16[768,128]{1,0:T(8,128)(2,1)S(1)} %collective-permute-done.5.refs_3_), channel_id=1, source_target_pairs={{0,64},{64,128},{128,192},{192,256},{256,320},{320,384},{384,448},... | collective-permute-start | bytes 589832 | tf_op jit(solution)/shard_map/ppermute | solution.py:393
  69.2 8.7 %collective-permute-start.1 = (bf16[768,128]{1,0:T(8,128)(2,1)S(1)}, bf16[768,128]{1,0:T(8,128)(2,1)S(1)}, u32[]{:S(2)}, u32[]{:S(2)}) collective-permute-start(bf16[768,128]{1,0:T(8,128)(2,1)S(1)} %collective-permute-done.refs_6_), channel_id=1, source_target_pairs={{0,64},{64,128},{128,192},{192,256},{256,320},{320,384},{384,448},... | collective-permute-start | bytes 589832 | tf_op jit(solution)/shard_map/ppermute | solution.py:394
  70.5 8.8 %collective-permute-start.4 = (bf16[96,512]{1,0:T(8,128)(2,1)S(1)}, bf16[96,512]{1,0:T(8,128)(2,1)S(1)}, u32[]{:S(2)}, u32[]{:S(2)}) collective-permute-start(bf16[96,512]{1,0:T(8,128)(2,1)S(1)} %get-tuple-element.19), channel_id=1, source_target_pairs={{0,8},{8,0},{16,24},{24,16},{32,40},{40,32},{48,56},{56,48},{64,72... | collective-permute-start | bytes 294920 | tf_op jit(solution)/shard_map/ppermute | solution.py:397
  76.6 6.4 %collective-permute-start.7 = (bf16[768,128]{1,0:T(8,128)(2,1)S(1)}, bf16[768,128]{1,0:T(8,128)(2,1)S(1)}, u32[]{:S(2)}, u32[]{:S(2)}) collective-permute-start(bf16[768,128]{1,0:T(8,128)(2,1)S(1)} %collective-permute-done.6.refs_4_), channel_id=1, source_target_pairs={{0,64},{64,128},{128,192},{192,256},{256,320},{320,384},{384,448},... | collective-permute-start | bytes 589832 | tf_op jit(solution)/shard_map/ppermute | solution.py:393
  77.9 7.2 %collective-permute-start.2 = (bf16[768,128]{1,0:T(8,128)(2,1)S(1)}, bf16[768,128]{1,0:T(8,128)(2,1)S(1)}, u32[]{:S(2)}, u32[]{:S(2)}) collective-permute-start(bf16[768,128]{1,0:T(8,128)(2,1)S(1)} %collective-permute-done.1.refs_7_), channel_id=1, source_target_pairs={{0,64},{64,128},{128,192},{192,256},{256,320},{320,384},{384,448},... | collective-permute-start | bytes 589832 | tf_op jit(solution)/shard_map/ppermute | solution.py:394
  83.1 6.4 %collective-permute-start.8 = (bf16[768,128]{1,0:T(8,128)(2,1)S(1)}, bf16[768,128]{1,0:T(8,128)(2,1)S(1)}, u32[]{:S(2)}, u32[]{:S(2)}) collective-permute-start(bf16[768,128]{1,0:T(8,128)(2,1)S(1)} %collective-permute-done.7.refs_5_), channel_id=1, source_target_pairs={{0,64},{64,128},{128,192},{192,256},{256,320},{320,384},{384,448},... | collective-permute-start | bytes 589832 | tf_op jit(solution)/shard_map/ppermute | solution.py:393
  85.2 6.5 %collective-permute-start.3 = (bf16[768,128]{1,0:T(8,128)(2,1)S(1)}, bf16[768,128]{1,0:T(8,128)(2,1)S(1)}, u32[]{:S(2)}, u32[]{:S(2)}) collective-permute-start(bf16[768,128]{1,0:T(8,128)(2,1)S(1)} %collective-permute-done.2.refs_8_), channel_id=1, source_target_pairs={{0,64},{64,128},{128,192},{192,256},{256,320},{320,384},{384,448},... | collective-permute-start | bytes 589832 | tf_op jit(solution)/shard_map/ppermute | solution.py:394

commit v6 on v5

--- a/solution.py
+++ b/solution.py
@@ -444,10 +444,8 @@
     others = lax.all_gather(
         second, "ctx", axis_index_groups=[[i, i + 1] for i in range(0, n, 2)], axis=0
     )
-    return jnp.where(
-        even,
-        jnp.concatenate([first, others[1]], axis=0),
-        jnp.concatenate([others[0], first], axis=0),
+    return lax.dynamic_update_slice(
+        others.reshape(tok, width), first, (jnp.where(even, 0, half), 0)
     )
 
 

time: 98.3 us -> 98.3 us (level)
  waiting for transfers between devices: 35.3 us -> 34.2 us
  Pallas kernels: 7.3 us -> 8.35 us
    pallas_call x2, Pallas kernels: 2.34 us -> 3.39 us  [attend(): pl.pallas_call(functools.partial(attend_kernel, n, groups, steps), out_sh...]
    ppermute x4, waiting for transfers between devices: 8.26 us -> 7.2 us  [local(): run_keys.append(lax.ppermute(run_keys[step], 'ctx', chain))]
  transfers between devices with their start and end apart: 10 -> 10, of which waited for: 7 -> 7; matrix products, arithmetic and copies ran while one was open for 0% -> 0% of each run, Pallas kernels for 3% -> 4%
where the time goes in v6:
time: 98.3 us; the launch traced here: 97.8 us
  waiting for transfers between devices  34.2 us (35%)
  starting transfers between devices  34.1 us (35%)
  blocking collectives  20.1 us (20%)
  Pallas kernels  8.35 us (8%)
    all_to_all x1, waiting for transfers between devices, local(): lax.all_to_all(packed.reshape(n, SLOTS, lanes), 'ctx', 0, 0, tiled=True)  23.8 us
    all_to_all x1, starting transfers between devices, local(): lax.all_to_all(packed.reshape(n, SLOTS, lanes), 'ctx', 0, 0, tiled=True)  17.6 us
    all_gather x1, blocking collectives, local(): lax.all_gather(my_kv, 'ctx', axis_index_groups=groups_of, axis=0, tiled=T...  15.3 us
    ppermute x4, waiting for transfers between devices, local(): run_keys.append(lax.ppermute(run_keys[step], 'ctx', chain))  7.2 us
    ppermute x1, starting transfers between devices, local(): taken = lax.ppermute(give, 'ctx', swap)  6.15 us
    ppermute x4, starting transfers between devices, local(): run_keys.append(lax.ppermute(run_keys[step], 'ctx', chain))  5.15 us
    ppermute x4, starting transfers between devices, local(): run_values.append(lax.ppermute(run_values[step], 'ctx', chain))  5.15 us
    all_gather x1, blocking collectives, local(): lax.all_gather(second, 'ctx', axis_index_groups=[[i, i + 1] for i in rang...  4.74 us
  transfers between devices with their start and end apart: 10, of which 7 were waited for; matrix products, arithmetic and copies ran while one was open for 0% of the time, Pallas kernels for 4%

profile of v6, /device:TPU:1, one launch (start us, length us, event | category | flops | bytes accessed | tf_op | source)
XLA Modules:
  0.0 97.8 jit_solution(2004824088838789783)
XLA Ops:
  0.0 2.6 %pack.1 = bf16[512,640]{1,0:T(8,128)(2,1)} custom-call(s32[1,192]{1,0:T(1,128)} %bitcast.17, bf16[192,512]{1,0:T(8,128)(2,1)} %q_hbm.1, bf16[192,128]{1,0:T(8,128)(2,1)} %k_hbm.1, bf16[192,128]{1,0:T(8,128)(2,1)} %v_hbm.1), custom_call_target="tpu_custom_call" | custom-call | tf_op jit(solution)/shard_map/pack/pallas_call | solution.py:353
  2.6 17.6 %all-to-all-start = ((bf16[64,8,640]{2,1,0:T(8,128)(2,1)}), bf16[64,8,640]{2,1,0:T(8,128)(2,1)S(1)}, u32[]{:S(2)}, u32[]{:S(2)}) async-start(bf16[64,8,640]{2,1,0:T(8,128)(2,1)} %bitcast.15), calls=%async_computation | async-start | bytes 1310720 | tf_op jit(solution)/shard_map/all_to_all | solution.py:368
  20.2 0.0 copy-start
  20.3 23.8 %all-to-all-done = bf16[64,8,640]{2,1,0:T(8,128)(2,1)S(1)} async-done(((bf16[64,8,640]{2,1,0:T(8,128)(2,1)}), bf16[64,8,640]{2,1,0:T(8,128)(2,1)S(1)}, u32[]{:S(2)}, u32[]{:S(2)}) %all-to-all-start) | async-done | bytes 655392 | tf_op jit(solution)/shard_map/all_to_all | solution.py:368
  44.0 1.2 %unpack.1 = (bf16[192,256]{1,0:T(8,128)(2,1)S(1)}, bf16[96,512]{1,0:T(8,128)(2,1)S(1)}, bf16[96,512]{1,0:T(8,128)(2,1)S(1)}) custom-call(s32[1]{0:T(128)} %bitcast.index_ref, bf16[512,640]{1,0:T(8,128)(2,1)S(1)} %bitcast.12), custom_call_target="tpu_custom_call" | custom-call | tf_op jit(solution)/shard_map/unpack/pallas_call | solution.py:372
  45.2 15.3 %all_gather.9 = bf16[1536,256]{1,0:T(8,128)(2,1)S(1)} all-gather(bf16[192,256]{1,0:T(8,128)(2,1)S(1)} %get-tuple-element.17), channel_id=1, replica_groups={{0,8,16,24,32,40,48,56},{64,72,80,88,96,104,112,120},{128,136,144,152,1..., dimensions={0}, use_global_device_ids=true | all-gather | bytes 884736 | tf_op jit(solution)/shard_map/all_gather | solution.py:383
  60.6 0.1 fusion
  60.7 1.3 %collective-permute-start.5 = (bf16[768,128]{1,0:T(8,128)(2,1)S(1)}, bf16[768,128]{1,0:T(8,128)(2,1)S(1)}, u32[]{:S(2)}, u32[]{:S(2)}) collective-permute-start(bf16[768,128]{1,0:T(8,128)(2,1)S(1)} %get-tuple-element.29.refs_2_), channel_id=1, source_target_pairs={{0,64},{64,128},{128,192},{192,256},{256,320},{320,384},{384,448},... | collective-permute-start | bytes 589832 | tf_op jit(solution)/shard_map/ppermute | solution.py:393
  62.0 1.3 %collective-permute-start = (bf16[768,128]{1,0:T(8,128)(2,1)S(1)}, bf16[768,128]{1,0:T(8,128)(2,1)S(1)}, u32[]{:S(2)}, u32[]{:S(2)}) collective-permute-start(bf16[768,128]{1,0:T(8,128)(2,1)S(1)} %get-tuple-element.30.refs_3_), channel_id=1, source_target_pairs={{0,64},{64,128},{128,192},{192,256},{256,320},{320,384},{384,448},... | collective-permute-start | bytes 589832 | tf_op jit(solution)/shard_map/ppermute | solution.py:394
  63.3 3.8 %collective-permute-done.5.refs_3_ = bf16[768,128]{1,0:T(8,128)(2,1)S(1)} collective-permute-done((bf16[768,128]{1,0:T(8,128)(2,1)S(1)}, bf16[768,128]{1,0:T(8,128)(2,1)S(1)}, u32[]{:S(2)}, u32[]{:S(2)}) %collective-permute-start.5) | collective-permute-done | bytes 196640 | tf_op jit(solution)/shard_map/ppermute | solution.py:393
  67.1 1.3 %collective-permute-start.6 = (bf16[768,128]{1,0:T(8,128)(2,1)S(1)}, bf16[768,128]{1,0:T(8,128)(2,1)S(1)}, u32[]{:S(2)}, u32[]{:S(2)}) collective-permute-start(bf16[768,128]{1,0:T(8,128)(2,1)S(1)} %collective-permute-done.5.refs_3_), channel_id=1, source_target_pairs={{0,64},{64,128},{128,192},{192,256},{256,320},{320,384},{384,448},... | collective-permute-start | bytes 589832 | tf_op jit(solution)/shard_map/ppermute | solution.py:393
  68.4 0.8 collective-permute-done.refs_6_
  69.2 1.3 %collective-permute-start.1 = (bf16[768,128]{1,0:T(8,128)(2,1)S(1)}, bf16[768,128]{1,0:T(8,128)(2,1)S(1)}, u32[]{:S(2)}, u32[]{:S(2)}) collective-permute-start(bf16[768,128]{1,0:T(8,128)(2,1)S(1)} %collective-permute-done.refs_6_), channel_id=1, source_target_pairs={{0,64},{64,128},{128,192},{192,256},{256,320},{320,384},{384,448},... | collective-permute-start | bytes 589832 | tf_op jit(solution)/shard_map/ppermute | solution.py:394
  70.5 6.1 %collective-permute-start.4 = (bf16[96,512]{1,0:T(8,128)(2,1)S(1)}, bf16[96,512]{1,0:T(8,128)(2,1)S(1)}, u32[]{:S(2)}, u32[]{:S(2)}) collective-permute-start(bf16[96,512]{1,0:T(8,128)(2,1)S(1)} %get-tuple-element.19), channel_id=1, source_target_pairs={{0,8},{8,0},{16,24},{24,16},{32,40},{40,32},{48,56},{56,48},{64,72... | collective-permute-start | bytes 294920 | tf_op jit(solution)/shard_map/ppermute | solution.py:397
  76.7 0.0 collective-permute-done.6.refs_4_
  76.7 1.3 %collective-permute-start.7 = (bf16[768,128]{1,0:T(8,128)(2,1)S(1)}, bf16[768,128]{1,0:T(8,128)(2,1)S(1)}, u32[]{:S(2)}, u32[]{:S(2)}) collective-permute-start(bf16[768,128]{1,0:T(8,128)(2,1)S(1)} %collective-permute-done.6.refs_4_), channel_id=1, source_target_pairs={{0,64},{64,128},{128,192},{192,256},{256,320},{320,384},{384,448},... | collective-permute-start | bytes 589832 | tf_op jit(solution)/shard_map/ppermute | solution.py:393
  78.0 0.0 collective-permute-done.1.refs_7_
  78.0 1.3 %collective-permute-start.2 = (bf16[768,128]{1,0:T(8,128)(2,1)S(1)}, bf16[768,128]{1,0:T(8,128)(2,1)S(1)}, u32[]{:S(2)}, u32[]{:S(2)}) collective-permute-start(bf16[768,128]{1,0:T(8,128)(2,1)S(1)} %collective-permute-done.1.refs_7_), channel_id=1, source_target_pairs={{0,64},{64,128},{128,192},{192,256},{256,320},{320,384},{384,448},... | collective-permute-start | bytes 589832 | tf_op jit(solution)/shard_map/ppermute | solution.py:394
  79.3 0.0 collective-permute-done.4.refs_1_
  79.3 0.0 copy-done
  79.3 1.6 %attend0.1 = (bf16[768,256]{1,0:T(8,128)(2,1)S(1)}, f32[768,128]{1,0:T(8,128)S(1)}, f32[768,256]{1,0:T(8,128)S(1)}) custom-call(s32[16]{0:T(128)S(1)} %copy-done, s32[1]{0:T(128)} %bitcast.index_ref, bf16[96,512]{1,0:T(8,128)(2,1)S(1)} %get-tuple-element.18.refs_0_, bf16[96,512]{1,0:T(8,128)(2,1)S(1)} %collective-permute-done.4.refs_1_, ...), custom_call_target="tpu_custom_call" | custom-call | flops 4831838208 | bytes 8388608 | tf_op jit(solution)/shard_map/attend0/pallas_call | solution.py:410
  80.9 2.2 %collective-permute-done.7.refs_5_ = bf16[768,128]{1,0:T(8,128)(2,1)S(1)} collective-permute-done((bf16[768,128]{1,0:T(8,128)(2,1)S(1)}, bf16[768,128]{1,0:T(8,128)(2,1)S(1)}, u32[]{:S(2)}, u32[]{:S(2)}) %collective-permute-start.7) | collective-permute-done | bytes 196640 | tf_op jit(solution)/shard_map/ppermute | solution.py:393
  83.1 1.3 %collective-permute-start.8 = (bf16[768,128]{1,0:T(8,128)(2,1)S(1)}, bf16[768,128]{1,0:T(8,128)(2,1)S(1)}, u32[]{:S(2)}, u32[]{:S(2)}) collective-permute-start(bf16[768,128]{1,0:T(8,128)(2,1)S(1)} %collective-permute-done.7.refs_5_), channel_id=1, source_target_pairs={{0,64},{64,128},{128,192},{192,256},{256,320},{320,384},{384,448},... | collective-permute-start | bytes 589832 | tf_op jit(solution)/shard_map/ppermute | solution.py:393
  84.4 0.8 collective-permute-done.2.refs_8_
  85.2 1.3 %collective-permute-start.3 = (bf16[768,128]{1,0:T(8,128)(2,1)S(1)}, bf16[768,128]{1,0:T(8,128)(2,1)S(1)}, u32[]{:S(2)}, u32[]{:S(2)}) collective-permute-start(bf16[768,128]{1,0:T(8,128)(2,1)S(1)} %collective-permute-done.2.refs_8_), channel_id=1, source_target_pairs={{0,64},{64,128},{128,192},{192,256},{256,320},{320,384},{384,448},... | collective-permute-start | bytes 589832 | tf_op jit(solution)/shard_map/ppermute | solution.py:394
  86.5 1.8 %attend1.1 = (f32[768,128]{1,0:T(8,128)S(1)}, f32[768,256]{1,0:T(8,128)S(1)}) custom-call(s32[16]{0:T(128)S(1)} %copy-done, s32[1]{0:T(128)} %bitcast.index_ref, bf16[768,256]{1,0:T(8,128)(2,1)S(1)} %get-tuple-element.20.refs_0_.heads_ref, f32[768,128]{1,0:T(8,128)S(1)} %get-tuple-element.21.refs_1_, f32[768,256]{1,0:T(8,128)S(1)} %get-tuple-element.22.refs_2_, ...), custom_call_target="tpu_custom_call" | custom-call | flops 14495514624 | bytes 8388608 | tf_op jit(solution)/shard_map/attend1/pallas_call | solution.py:410
  88.3 1.2 %collective-permute-done.8.key_ref = bf16[768,128]{1,0:T(8,128)(2,1)S(1)} collective-permute-done((bf16[768,128]{1,0:T(8,128)(2,1)S(1)}, bf16[768,128]{1,0:T(8,128)(2,1)S(1)}, u32[]{:S(2)}, u32[]{:S(2)}) %collective-permute-start.8) | collective-permute-done | bytes 196640 | tf_op jit(solution)/shard_map/ppermute | solution.py:393
  89.5 0.6 far_score.1
  90.1 1.6 %collective-permute-done.3.value_ref = bf16[768,128]{1,0:T(8,128)(2,1)S(1)} collective-permute-done((bf16[768,128]{1,0:T(8,128)(2,1)S(1)}, bf16[768,128]{1,0:T(8,128)(2,1)S(1)}, u32[]{:S(2)}, u32[]{:S(2)}) %collective-permute-start.3) | collective-permute-done | bytes 196640 | tf_op jit(solution)/shard_map/ppermute | solution.py:394
  91.7 0.6 finish.1
  92.4 4.7 %all-gather = bf16[192,512]{1,0:T(8,128)(2,1)S(1)} all-gather(bf16[96,512]{1,0:T(8,128)(2,1)S(1)} %get-tuple-element.27), channel_id=2, replica_groups={{0,8},{16,24},{32,40},{48,56},{64,72},{80,88},{96,104},{112,120},{128,1..., dimensions={0}, use_global_device_ids=true | all-gather | bytes 294912 | tf_op jit(solution)/shard_map/all_gather | solution.py:444
  97.1 0.7 copy.12
  (3 shorter events, 0.1 us)
Async XLA Ops:
  2.6 41.4 %all-to-all-start = ((bf16[64,8,640]{2,1,0:T(8,128)(2,1)}), bf16[64,8,640]{2,1,0:T(8,128)(2,1)S(1)}, u32[]{:S(2)}, u32[]{:S(2)}) async-start(bf16[64,8,640]{2,1,0:T(8,128)(2,1)} %bitcast.15), calls=%async_computation | async-start | bytes 1310720 | tf_op jit(solution)/shard_map/all_to_all | solution.py:368
  20.2 59.1 %copy-start = (s32[16]{0:T(128)S(1)}, s32[16]{0:T(128)}, u32[]{:S(2)}) copy-start(s32[16]{0:T(128)} %lengths_ref.7) | copy-start | bytes 196
  60.7 6.4 %collective-permute-start.5 = (bf16[768,128]{1,0:T(8,128)(2,1)S(1)}, bf16[768,128]{1,0:T(8,128)(2,1)S(1)}, u32[]{:S(2)}, u32[]{:S(2)}) collective-permute-start(bf16[768,128]{1,0:T(8,128)(2,1)S(1)} %get-tuple-element.29.refs_2_), channel_id=1, source_target_pairs={{0,64},{64,128},{128,192},{192,256},{256,320},{320,384},{384,448},... | collective-permute-start | bytes 589832 | tf_op jit(solution)/shard_map/ppermute | solution.py:393
  62.0 7.2 %collective-permute-start = (bf16[768,128]{1,0:T(8,128)(2,1)S(1)}, bf16[768,128]{1,0:T(8,128)(2,1)S(1)}, u32[]{:S(2)}, u32[]{:S(2)}) collective-permute-start(bf16[768,128]{1,0:T(8,128)(2,1)S(1)} %get-tuple-element.30.refs_3_), channel_id=1, source_target_pairs={{0,64},{64,128},{128,192},{192,256},{256,320},{320,384},{384,448},... | collective-permute-start | bytes 589832 | tf_op jit(solution)/shard_map/ppermute | solution.py:394
  67.1 9.6 %collective-permute-start.6 = (bf16[768,128]{1,0:T(8,128)(2,1)S(1)}, bf16[768,128]{1,0:T(8,128)(2,1)S(1)}, u32[]{:S(2)}, u32[]{:S(2)}) collective-permute-start(bf16[768,128]{1,0:T(8,128)(2,1)S(1)} %collective-permute-done.5.refs_3_), channel_id=1, source_target_pairs={{0,64},{64,128},{128,192},{192,256},{256,320},{320,384},{384,448},... | collective-permute-start | bytes 589832 | tf_op jit(solution)/shard_map/ppermute | solution.py:393
  69.2 8.8 %collective-permute-start.1 = (bf16[768,128]{1,0:T(8,128)(2,1)S(1)}, bf16[768,128]{1,0:T(8,128)(2,1)S(1)}, u32[]{:S(2)}, u32[]{:S(2)}) collective-permute-start(bf16[768,128]{1,0:T(8,128)(2,1)S(1)} %collective-permute-done.refs_6_), channel_id=1, source_target_pairs={{0,64},{64,128},{128,192},{192,256},{256,320},{320,384},{384,448},... | collective-permute-start | bytes 589832 | tf_op jit(solution)/shard_map/ppermute | solution.py:394
  70.5 8.8 %collective-permute-start.4 = (bf16[96,512]{1,0:T(8,128)(2,1)S(1)}, bf16[96,512]{1,0:T(8,128)(2,1)S(1)}, u32[]{:S(2)}, u32[]{:S(2)}) collective-permute-start(bf16[96,512]{1,0:T(8,128)(2,1)S(1)} %get-tuple-element.19), channel_id=1, source_target_pairs={{0,8},{8,0},{16,24},{24,16},{32,40},{40,32},{48,56},{56,48},{64,72... | collective-permute-start | bytes 294920 | tf_op jit(solution)/shard_map/ppermute | solution.py:397
  76.7 6.4 %collective-permute-start.7 = (bf16[768,128]{1,0:T(8,128)(2,1)S(1)}, bf16[768,128]{1,0:T(8,128)(2,1)S(1)}, u32[]{:S(2)}, u32[]{:S(2)}) collective-permute-start(bf16[768,128]{1,0:T(8,128)(2,1)S(1)} %collective-permute-done.6.refs_4_), channel_id=1, source_target_pairs={{0,64},{64,128},{128,192},{192,256},{256,320},{320,384},{384,448},... | collective-permute-start | bytes 589832 | tf_op jit(solution)/shard_map/ppermute | solution.py:393
  78.0 7.2 %collective-permute-start.2 = (bf16[768,128]{1,0:T(8,128)(2,1)S(1)}, bf16[768,128]{1,0:T(8,128)(2,1)S(1)}, u32[]{:S(2)}, u32[]{:S(2)}) collective-permute-start(bf16[768,128]{1,0:T(8,128)(2,1)S(1)} %collective-permute-done.1.refs_7_), channel_id=1, source_target_pairs={{0,64},{64,128},{128,192},{192,256},{256,320},{320,384},{384,448},... | collective-permute-start | bytes 589832 | tf_op jit(solution)/shard_map/ppermute | solution.py:394
  83.1 6.4 %collective-permute-start.8 = (bf16[768,128]{1,0:T(8,128)(2,1)S(1)}, bf16[768,128]{1,0:T(8,128)(2,1)S(1)}, u32[]{:S(2)}, u32[]{:S(2)}) collective-permute-start(bf16[768,128]{1,0:T(8,128)(2,1)S(1)} %collective-permute-done.7.refs_5_), channel_id=1, source_target_pairs={{0,64},{64,128},{128,192},{192,256},{256,320},{320,384},{384,448},... | collective-permute-start | bytes 589832 | tf_op jit(solution)/shard_map/ppermute | solution.py:393
  85.2 6.5 %collective-permute-start.3 = (bf16[768,128]{1,0:T(8,128)(2,1)S(1)}, bf16[768,128]{1,0:T(8,128)(2,1)S(1)}, u32[]{:S(2)}, u32[]{:S(2)}) collective-permute-start(bf16[768,128]{1,0:T(8,128)(2,1)S(1)} %collective-permute-done.2.refs_8_), channel_id=1, source_target_pairs={{0,64},{64,128},{128,192},{192,256},{256,320},{320,384},{384,448},... | collective-permute-start | bytes 589832 | tf_op jit(solution)/shard_map/ppermute | solution.py:394
